TPU v7x, 128 devices: a whole 4x4x4 slice. The times are simulated.
128 devices in a mesh: ctx: 16 (over x, z_hi, core), exp: 8 (over y, z_lo).
Axes of the slice: x: 4, y: 4, z: 4 (z_hi: 2, z_lo: 2; z = z_hi * 2 + z_lo), core: 2. Of those that a mesh axis runs over, the one named last changes fastest.
Arguments:
- queries: bfloat16 [128, 36864], P('ctx', 'exp'), may hold values from -82.5 to 82.5
- latents: bfloat16 [16384, 576], P('ctx'), may hold values from -4.5 to 4.5
- out_grad: bfloat16 [128, 32768], P('ctx', 'exp'), may hold values from -6 to 6
- hidden_rows: bfloat16 [16384, 5120], P(('ctx', 'exp')), may hold values from -6 to 6
- norm_gain: float32 [5120], replicated, may hold values from 0.25 to 4
- latent_proj: bfloat16 [5120, 576], replicated, may hold values from -0.078125 to 0.078125
- stream_grad: bfloat16 [16384, 5120], P(('ctx', 'exp')), may hold values from -6 to 6
- expert_ids: int32 [16384, 2], P(('ctx', 'exp')), may hold values from 0 to 7, all different within a row; in each aligned block of 128 rows (0 to 127, 128 to 255, ...) at most 64 rows name the same one
- route_weights: float32 [16384, 2], P(('ctx', 'exp')), may hold values from 0.1 to 1
- expert_acts: bfloat16 [8, 8192, 768], P('exp', 'ctx'), may hold values from -6 to 6
- down_proj: bfloat16 [8, 768, 5120], P('exp'), may hold values from -0.21875 to 0.21875
Outputs:
- query_grad: bfloat16 [128, 36864], P('ctx', 'exp')
- stream_total: bfloat16 [16384, 5120], P(('ctx', 'exp'))
- act_grad: bfloat16 [8, 8192, 768], P('exp', 'ctx')
- down_grad: bfloat16 [8, 768, 5120], P('exp', 'ctx')
- weight_grad: float32 [16384, 2], P(('ctx', 'exp'))
Inputs may be any that keep to these rules, and one draw needn't show every extreme that they name: `expert_ids`: within the rows of one device no expert is named more than 64 times.
All inputs are finite; a program needn't handle non-finite values.
Results may differ from a plain program's by a relative error of at most 0.03.
Values may be sent and summed in bfloat16 or wider, within the bound.
A program may use at most 128 MiB of HBM per device.

v0:
```python
import jax
import jax.numpy as jnp
from jax import lax
from jax.sharding import PartitionSpec as P

EPSILON = 1e-06
NEG_LARGE = -1e30


def from_behind(block, axis, distance):
    devices = range(lax.axis_size(axis))
    route = [((i - distance) % len(devices), i) for i in devices]
    return lax.ppermute(block, axis, route)


def block_terms(query_heads, grad_heads, key_block, key_pos, query_pos, score_scale):
    value_width = grad_heads.shape[2]
    scores = (
        jnp.einsum("qhk,nk->hqn", query_heads, key_block, preferred_element_type=jnp.float32)
        * score_scale
    )
    prob_grads = jnp.einsum(
        "qhl,nl->hqn", grad_heads, key_block[:, :value_width], preferred_element_type=jnp.float32
    )
    visible = (key_pos[None, :] <= query_pos[:, None])[None]
    masked = jnp.where(visible, scores, NEG_LARGE)
    return (masked, prob_grads, visible)


def forward_update(stats_now, query_heads, grad_heads, key_block, key_pos, query_pos, score_scale):
    running_max, running_sum, running_dot = stats_now
    masked, prob_grads, visible = block_terms(
        query_heads, grad_heads, key_block, key_pos, query_pos, score_scale
    )
    new_max = jnp.maximum(running_max, jnp.max(masked, axis=-1))
    weights = jnp.where(visible, jnp.exp(masked - new_max[..., None]), 0.0)
    factor = jnp.exp(running_max - new_max)
    new_sum = running_sum * factor + jnp.sum(weights, axis=-1)
    new_dot = running_dot * factor + jnp.sum(weights * prob_grads, axis=-1)
    return (new_max, new_sum, new_dot)


def backward_block(
    query_heads, grad_heads, key_block, key_pos, query_pos, score_scale, log_total, row_delta
):
    masked, prob_grads, visible = block_terms(
        query_heads, grad_heads, key_block, key_pos, query_pos, score_scale
    )
    probs_now = jnp.where(visible, jnp.exp(masked - log_total[..., None]), 0.0)
    score_grads = (probs_now * (prob_grads - row_delta[..., None])).astype(jnp.bfloat16)
    query_add = (
        jnp.einsum("hqn,nk->qhk", score_grads, key_block, preferred_element_type=jnp.float32)
        * score_scale
    )
    key_add = (
        jnp.einsum("hqn,qhk->nk", score_grads, query_heads, preferred_element_type=jnp.float32)
        * score_scale
    )
    value_add = jnp.einsum(
        "hqn,qhl->nl",
        probs_now.astype(jnp.bfloat16),
        grad_heads,
        preferred_element_type=jnp.float32,
    )
    key_add = key_add + jnp.pad(value_add, ((0, 0), (0, key_block.shape[1] - value_add.shape[1])))
    return (query_add, key_add)


def finish_stats(stats_now):
    running_max, running_sum, running_dot = stats_now
    return (running_max + jnp.log(running_sum), running_dot / running_sum)


def body(
    queries,
    latents,
    out_grad,
    hidden_rows,
    norm_gain,
    latent_proj,
    stream_grad,
    expert_ids,
    route_weights,
    expert_acts,
    down_proj,
):
    key_count = latents.shape[0]
    key_width = latents.shape[1]
    query_rows = queries.shape[0]
    head_count = queries.shape[1] // key_width
    value_width = out_grad.shape[1] // head_count
    query_heads = queries.reshape(query_rows, head_count, key_width)
    grad_heads = out_grad.reshape(query_rows, head_count, value_width)
    score_scale = key_width ** (-0.5)
    cycle_size = lax.axis_size("ctx")
    cycle_index = lax.axis_index("ctx")
    key_pos = cycle_index * key_count + jnp.arange(key_count, dtype=jnp.int32)
    zero_rows = jnp.zeros((head_count, query_rows), jnp.float32)
    query_zero = jnp.zeros((query_rows, head_count, key_width), jnp.float32)
    key_zero = jnp.zeros((key_count, key_width), jnp.float32)

    def query_positions(anchor):
        return anchor * key_count + key_count - query_rows + jnp.arange(query_rows, dtype=jnp.int32)

    def rotate_queries(packet):
        return from_behind((packet[0], packet[1]), "ctx", 1)

    def rotate_stats(stats_now):
        return from_behind(stats_now, "ctx", 1)

    def rotate_grads(carried):
        return from_behind((carried[0], carried[1], carried[2]), "ctx", 1)

    def anchor_of(turn_index):
        return (cycle_index - turn_index) % cycle_size

    def forward_visit(turn_index, packet, stats_now):
        anchor = anchor_of(turn_index)

        def forward_compute(stats_in):
            return forward_update(
                stats_in,
                packet[0],
                packet[1],
                latents,
                key_pos,
                query_positions(anchor),
                score_scale,
            )

        return lax.cond(
            cycle_index <= anchor, forward_compute, lambda stats_in: stats_in, stats_now
        )

    def forward_turn(turn_index, loop_state):
        packet, stats_now = loop_state
        stats_now = forward_visit(turn_index, packet, stats_now)
        return (rotate_queries(packet), rotate_stats(stats_now))

    start_stats = (jnp.full((head_count, query_rows), NEG_LARGE, jnp.float32), zero_rows, zero_rows)
    packet, stats_now = lax.fori_loop(
        0, cycle_size - 1, forward_turn, ((query_heads, grad_heads), start_stats)
    )
    stats_now = rotate_stats(forward_visit(cycle_size - 1, packet, stats_now))
    log_total, row_delta = finish_stats(stats_now)

    def backward_visit(turn_index, packet, carried, key_acc):
        log_in, delta_in, query_in = carried
        anchor = anchor_of(turn_index)

        def backward_compute(totals):
            query_add, key_add = backward_block(
                packet[0],
                packet[1],
                latents,
                key_pos,
                query_positions(anchor),
                score_scale,
                log_in,
                delta_in,
            )
            return (totals[0] + query_add, totals[1] + key_add)

        query_in, key_acc = lax.cond(
            cycle_index <= anchor, backward_compute, lambda totals: totals, (query_in, key_acc)
        )
        return ((log_in, delta_in, query_in), key_acc)

    def backward_turn(turn_index, loop_state):
        packet, carried, key_acc = loop_state
        carried, key_acc = backward_visit(turn_index, packet, carried, key_acc)
        return (rotate_queries(packet), rotate_grads(carried), key_acc)

    start_carried = (log_total, row_delta, query_zero)
    packet, carried, key_acc = lax.fori_loop(
        0, cycle_size - 1, backward_turn, ((query_heads, grad_heads), start_carried, key_zero)
    )
    carried, key_acc = backward_visit(cycle_size - 1, packet, carried, key_acc)
    carried = rotate_grads(carried)
    query_acc = carried[2]
    key_rows = lax.psum_scatter(
        key_acc.astype(jnp.bfloat16), "exp", scatter_dimension=0, tiled=True
    )
    query_grad = query_acc.astype(jnp.bfloat16).reshape(query_rows, head_count * key_width)
    norm_grad = lax.dot_general(
        key_rows, latent_proj, (((1,), (1,)), ((), ())), preferred_element_type=jnp.float32
    )
    row_values = hidden_rows.astype(jnp.float32)
    inverse = lax.rsqrt(jnp.mean(row_values * row_values, axis=-1, keepdims=True) + EPSILON)
    gained = norm_gain * norm_grad
    through_norm = inverse * gained - row_values * (inverse * inverse * inverse) * jnp.mean(
        row_values * gained, axis=-1, keepdims=True
    )
    stream_total = (stream_grad.astype(jnp.float32) + through_norm).astype(jnp.bfloat16)
    expert_count = lax.axis_size("exp")
    slot_count = expert_acts.shape[1]
    capacity = slot_count // expert_count
    local_rows = expert_ids.shape[0]
    top_count = expert_ids.shape[1]
    flat_ids = expert_ids.reshape(-1)
    chosen = (flat_ids[:, None] == jnp.arange(expert_count, dtype=jnp.int32)[None, :]).astype(
        jnp.int32
    )
    earlier = jnp.cumsum(chosen, axis=0) - chosen
    slot_of = flat_ids * capacity + jnp.sum(earlier * chosen, axis=1)
    select = (slot_of[:, None] == jnp.arange(slot_count, dtype=jnp.int32)[None, :]).astype(
        jnp.float32
    )
    select = select.reshape(local_rows, top_count, slot_count)
    placing = jnp.sum(select, axis=1).astype(jnp.bfloat16)
    outgoing = lax.dot_general(
        placing, stream_total, (((0,), (0,)), ((), ())), preferred_element_type=jnp.float32
    ).astype(jnp.bfloat16)
    rounded_weights = lax.optimization_barrier(route_weights.astype(jnp.bfloat16)).astype(
        jnp.float32
    )
    weight_slots = jnp.einsum("tks,tk->s", select, rounded_weights).astype(jnp.bfloat16)
    arrived, arrived_weights = (
        lax.all_to_all(
            outgoing.reshape(expert_count, capacity, -1),
            "exp",
            split_axis=0,
            concat_axis=0,
            tiled=True,
        ),
        lax.all_to_all(
            weight_slots.reshape(expert_count, capacity),
            "exp",
            split_axis=0,
            concat_axis=0,
            tiled=True,
        ),
    )
    arrived = arrived.reshape(slot_count, -1)
    arrived_weights = arrived_weights.reshape(slot_count)
    expert_rows = expert_acts[0]
    weight = down_proj[0]
    scaled = (arrived_weights.astype(jnp.float32)[:, None] * arrived.astype(jnp.float32)).astype(
        jnp.bfloat16
    )
    act_grad = lax.dot_general(
        scaled, weight, (((1,), (1,)), ((), ())), preferred_element_type=jnp.float32
    ).astype(jnp.bfloat16)
    outputs = jnp.dot(expert_rows, weight, preferred_element_type=jnp.float32)
    slot_grads = jnp.sum(arrived.astype(jnp.float32) * outputs, axis=1)
    returned = lax.all_to_all(
        slot_grads.reshape(expert_count, capacity), "exp", split_axis=0, concat_axis=0, tiled=True
    ).reshape(slot_count)
    weight_grad = jnp.einsum("tks,s->tk", select, returned)
    down_share = lax.psum_scatter(
        lax.dot_general(
            expert_rows, scaled, (((0,), (0,)), ((), ())), preferred_element_type=jnp.float32
        ).astype(jnp.bfloat16),
        "ctx",
        scatter_dimension=0,
        tiled=True,
    )
    return (query_grad, stream_total, act_grad[None], down_share[None], weight_grad)


def solution(mesh):
    in_specs = (
        P("ctx", "exp"),
        P("ctx", None),
        P("ctx", "exp"),
        P(("ctx", "exp"), None),
        P(),
        P(),
        P(("ctx", "exp"), None),
        P(("ctx", "exp"), None),
        P(("ctx", "exp"), None),
        P("exp", "ctx", None),
        P("exp", None, None),
    )
    out_specs = (
        P("ctx", "exp"),
        P(("ctx", "exp"), None),
        P("exp", "ctx", None),
        P("exp", "ctx", None),
        P(("ctx", "exp"), None),
    )
    return jax.shard_map(body, mesh=mesh, in_specs=in_specs, out_specs=out_specs, check_vma=False)
```

profile of v0, /device:TPU:0, one launch (start us, length us, event | category | flops | bytes accessed | tf_op | source)
XLA Modules:
  0.0 741.6 jit_solution(12814577714595886866)
XLA Ops:
  12.4 218.9 %while.50 = (s32[]{:T(128)}, bf16[8,8,576]{2,1,0:T(8,128)(2,1)S(1)}, bf16[8,8,512]{2,1,0:T(8,128)(2,1)S(1)}, f32[8,8]{0,1:T(8,128)S(1)}, f32[8,8]{0,1:T(8,128)S(...) while((s32[]{:T(128)}, ...), condition=%wide.region_6.7_spmd.clone, body=%wide.region_0.6_spmd.clone.sunk | while | flops 143271120 | bytes 4047524 | solution.py:141
  17.8 5.1 conditional.10
  23.7 6.1 collective-permute-done.3
  33.4 5.1 conditional.10
  38.7 6.7 collective-permute-done.3
  46.8 5.1 conditional.10
  52.2 6.7 collective-permute-done.3
  60.2 5.1 conditional.10
  65.6 6.7 collective-permute-done.3
  73.6 5.1 conditional.10
  79.0 6.7 collective-permute-done.3
  87.1 5.1 conditional.10
  92.4 6.7 collective-permute-done.3
  100.5 5.1 conditional.10
  105.8 6.7 collective-permute-done.3
  113.9 5.1 conditional.10
  119.2 6.7 collective-permute-done.3
  127.3 5.1 conditional.10
  144.1 5.1 conditional.10
  149.7 6.5 collective-permute-done.3
  157.5 5.1 conditional.10
  163.1 6.5 collective-permute-done.3
  171.0 5.1 conditional.10
  178.0 5.0 collective-permute-done.3
  185.9 5.1 conditional.10
  193.3 4.6 collective-permute-done.3
  201.2 5.1 conditional.10
  206.5 4.7 collective-permute-start.3
  213.3 4.6 collective-permute-done.4
  219.2 5.1 conditional.10
  224.7 6.5 collective-permute-done.3
  232.4 5.0 conditional.4
  237.6 6.7 collective-permute-done.10
  244.6 230.6 %while.51 = (s32[]{:T(128)}, bf16[8,8,576]{2,1,0:T(8,128)(2,1)S(1)}, bf16[8,8,512]{2,1,0:T(8,128)(2,1)}, f32[8,8]{0,1:T(8,128)S(1)}, f32[8,8]{0,1:T(8,128)S(1)},...) while((s32[]{:T(128)}, ...), condition=%wide.region_15.16_spmd.clone, body=%wide.region_12.15_spmd.clone.sunk | while | flops 363086848 | bytes 20553672 | solution.py:175
  252.2 6.2 collective-permute-done.9
  265.7 8.1 %collective-permute-done.9 = f32[8,8,576]{2,0,1:T(8,128)} collective-permute-done((f32[8,8,576]{2,0,1:T(8,128)S(1)}, f32[8,8,576]{2,0,1:T(8,128)}, u32[]{:S(2)}, u32[]{:S(2)}) %collective-permute-start.9) | collective-permute-done | bytes 147488 | tf_op jit(solution)/shard_map/while/body/eval_jaxpr/ppermute | solution.py:13
  281.1 8.1 %collective-permute-done.9 = f32[8,8,576]{2,0,1:T(8,128)} collective-permute-done((f32[8,8,576]{2,0,1:T(8,128)S(1)}, f32[8,8,576]{2,0,1:T(8,128)}, u32[]{:S(2)}, u32[]{:S(2)}) %collective-permute-start.9) | collective-permute-done | bytes 147488 | tf_op jit(solution)/shard_map/while/body/eval_jaxpr/ppermute | solution.py:13
  291.7 4.3 conditional.11
  296.4 8.1 %collective-permute-done.9 = f32[8,8,576]{2,0,1:T(8,128)} collective-permute-done((f32[8,8,576]{2,0,1:T(8,128)S(1)}, f32[8,8,576]{2,0,1:T(8,128)}, u32[]{:S(2)}, u32[]{:S(2)}) %collective-permute-start.9) | collective-permute-done | bytes 147488 | tf_op jit(solution)/shard_map/while/body/eval_jaxpr/ppermute | solution.py:13
  307.1 4.3 conditional.11
  311.8 8.1 %collective-permute-done.9 = f32[8,8,576]{2,0,1:T(8,128)} collective-permute-done((f32[8,8,576]{2,0,1:T(8,128)S(1)}, f32[8,8,576]{2,0,1:T(8,128)}, u32[]{:S(2)}, u32[]{:S(2)}) %collective-permute-start.9) | collective-permute-done | bytes 147488 | tf_op jit(solution)/shard_map/while/body/eval_jaxpr/ppermute | solution.py:13
  322.4 4.3 conditional.11
  327.2 8.1 %collective-permute-done.9 = f32[8,8,576]{2,0,1:T(8,128)} collective-permute-done((f32[8,8,576]{2,0,1:T(8,128)S(1)}, f32[8,8,576]{2,0,1:T(8,128)}, u32[]{:S(2)}, u32[]{:S(2)}) %collective-permute-start.9) | collective-permute-done | bytes 147488 | tf_op jit(solution)/shard_map/while/body/eval_jaxpr/ppermute | solution.py:13
  342.6 8.1 %collective-permute-done.9 = f32[8,8,576]{2,0,1:T(8,128)} collective-permute-done((f32[8,8,576]{2,0,1:T(8,128)S(1)}, f32[8,8,576]{2,0,1:T(8,128)}, u32[]{:S(2)}, u32[]{:S(2)}) %collective-permute-start.9) | collective-permute-done | bytes 147488 | tf_op jit(solution)/shard_map/while/body/eval_jaxpr/ppermute | solution.py:13
  357.9 8.1 %collective-permute-done.9 = f32[8,8,576]{2,0,1:T(8,128)} collective-permute-done((f32[8,8,576]{2,0,1:T(8,128)S(1)}, f32[8,8,576]{2,0,1:T(8,128)}, u32[]{:S(2)}, u32[]{:S(2)}) %collective-permute-start.9) | collective-permute-done | bytes 147488 | tf_op jit(solution)/shard_map/while/body/eval_jaxpr/ppermute | solution.py:13
  373.3 8.1 %collective-permute-done.9 = f32[8,8,576]{2,0,1:T(8,128)} collective-permute-done((f32[8,8,576]{2,0,1:T(8,128)S(1)}, f32[8,8,576]{2,0,1:T(8,128)}, u32[]{:S(2)}, u32[]{:S(2)}) %collective-permute-start.9) | collective-permute-done | bytes 147488 | tf_op jit(solution)/shard_map/while/body/eval_jaxpr/ppermute | solution.py:13
  388.7 8.1 %collective-permute-done.9 = f32[8,8,576]{2,0,1:T(8,128)} collective-permute-done((f32[8,8,576]{2,0,1:T(8,128)S(1)}, f32[8,8,576]{2,0,1:T(8,128)}, u32[]{:S(2)}, u32[]{:S(2)}) %collective-permute-start.9) | collective-permute-done | bytes 147488 | tf_op jit(solution)/shard_map/while/body/eval_jaxpr/ppermute | solution.py:13
  404.1 8.1 %collective-permute-done.9 = f32[8,8,576]{2,0,1:T(8,128)} collective-permute-done((f32[8,8,576]{2,0,1:T(8,128)S(1)}, f32[8,8,576]{2,0,1:T(8,128)}, u32[]{:S(2)}, u32[]{:S(2)}) %collective-permute-start.9) | collective-permute-done | bytes 147488 | tf_op jit(solution)/shard_map/while/body/eval_jaxpr/ppermute | solution.py:13
  419.4 8.1 %collective-permute-done.9 = f32[8,8,576]{2,0,1:T(8,128)} collective-permute-done((f32[8,8,576]{2,0,1:T(8,128)S(1)}, f32[8,8,576]{2,0,1:T(8,128)}, u32[]{:S(2)}, u32[]{:S(2)}) %collective-permute-start.9) | collective-permute-done | bytes 147488 | tf_op jit(solution)/shard_map/while/body/eval_jaxpr/ppermute | solution.py:13
  434.8 8.1 %collective-permute-done.9 = f32[8,8,576]{2,0,1:T(8,128)} collective-permute-done((f32[8,8,576]{2,0,1:T(8,128)S(1)}, f32[8,8,576]{2,0,1:T(8,128)}, u32[]{:S(2)}, u32[]{:S(2)}) %collective-permute-start.9) | collective-permute-done | bytes 147488 | tf_op jit(solution)/shard_map/while/body/eval_jaxpr/ppermute | solution.py:13
  450.2 8.1 %collective-permute-done.9 = f32[8,8,576]{2,0,1:T(8,128)} collective-permute-done((f32[8,8,576]{2,0,1:T(8,128)S(1)}, f32[8,8,576]{2,0,1:T(8,128)}, u32[]{:S(2)}, u32[]{:S(2)}) %collective-permute-start.9) | collective-permute-done | bytes 147488 | tf_op jit(solution)/shard_map/while/body/eval_jaxpr/ppermute | solution.py:13
  465.6 8.1 %collective-permute-done.9 = f32[8,8,576]{2,0,1:T(8,128)} collective-permute-done((f32[8,8,576]{2,0,1:T(8,128)S(1)}, f32[8,8,576]{2,0,1:T(8,128)}, u32[]{:S(2)}, u32[]{:S(2)}) %collective-permute-start.9) | collective-permute-done | bytes 147488 | tf_op jit(solution)/shard_map/while/body/eval_jaxpr/ppermute | solution.py:13
  475.3 10.4 %conditional.5 = ((f32[8,8,576]{2,0,1:T(8,128)S(1)}, f32[1024,576]{0,1:T(8,128)S(1)})) conditional(s32[]{:T(128)} %convert_element_type.115, (f32[8,8,576]{2,0,1:T(8,128)S(1)}, f32[1024,576]{0,1:T(8,128)S(1)}) %tuple.84, (s32[1024]{0:T(1024)}, s32[]{:T(128)}, bf16[1024,576]{0,1:T(8,128)(2,1)}, bf16[8,8,576]{2,1,0:T(8,128)(2,1)S(1)}, ...), branch_computations={%region_16.17_spmd, %region_17.18_spmd} | conditional | flops 363085824 | bytes 22221484 | solution.py:164
  492.0 4.9 all-to-all-start
  497.0 31.8 %reduce-scatter.7.cloned.1.call-done = bf16[128,576]{1,0:T(8,128)(2,1)} async-done(((bf16[1024,576]{1,0:T(8,128)(2,1)}), bf16[128,576]{1,0:T(8,128)(2,1)}) %reduce-scatter.7.cloned.1.call-update) | async-done | bytes 147472
  528.8 4.4 fusion.117
  537.9 4.7 all-to-all-start.1
  542.7 70.6 %all-to-all-done.1 = bf16[8,64,5120]{2,1,0:T(8,128)(2,1)} async-done(((bf16[8,64,5120]{2,1,0:T(8,128)(2,1)}), bf16[8,64,5120]{2,1,0:T(8,128)(2,1)}, u32[]{:S(2)}, u32[]{:S(2)}) %all-to-all-start.1) | async-done | bytes 5242912 | tf_op jit(solution)/shard_map/all_to_all | solution.py:219
  619.8 6.5 fusion.116
  626.3 10.6 %copy.159 = bf16[768,5120]{1,0:T(8,128)(2,1)} copy(bf16[768,5120]{0,1:T(8,128)(2,1)} %fusion.116) | data formatting | bytes 15728640
  637.0 7.5 %collective-permute-done.13 = bf16[8,8,576]{2,0,1:T(8,128)(2,1)S(1)} collective-permute-done((bf16[8,8,576]{2,0,1:T(8,128)(2,1)S(1)}, bf16[8,8,576]{2,0,1:T(8,128)(2,1)S(1)}, u32[]{:S(2)}, u32[]{:S(2)}) %collective-permute-start.13) | collective-permute-done | bytes 73760 | tf_op jit(solution)/shard_map/ppermute | solution.py:13
  645.3 9.5 %fusion.112 = f32[512]{0:T(512)S(1)} fusion(bf16[1,768,5120]{2,1,0:T(8,128)(2,1)} %param.33, bf16[8,64,5120]{2,1,0:T(8,128)(2,1)} %all-to-all-done.1, bf16[1,512,768]{2,1,0:T(8,128)(2,1)S(1)} %copy-done), kind=kOutput, calls=%fused_computation.91 | convolution fusion | flops 4034395648 | bytes 13895680 | tf_op jit(solution)/shard_map/dot_general | solution.py:244
  659.0 10.1 %fusion.126 = bf16[1,512,768]{2,1,0:T(8,128)(2,1)} fusion(bf16[512,5120]{1,0:T(8,128)(2,1)} %bitcast.233, bf16[1,768,5120]{2,1,0:T(8,128)(2,1)} %param.33), kind=kOutput, calls=%fused_computation.110 | convolution fusion | flops 4026925056 | bytes 13893632 | tf_op jit(solution)/shard_map/dot_general | solution.py:241
  671.2 60.7 %reduce-scatter.9.cloned.1.call-done = bf16[48,5120]{1,0:T(8,128)(2,1)} async-done(((bf16[768,5120]{1,0:T(8,128)(2,1)}), bf16[48,5120]{1,0:T(8,128)(2,1)}) %reduce-scatter.9.cloned.1.call-update) | async-done | bytes 491536
  (823 shorter events, 335.6 us)
Async XLA Ops:
  7.2 521.6 %reduce-scatter.7.cloned.1.call-start = ((), (), s32[]{:S(2)}) async-start(), calls=%async_computation.5 | async-start | bytes 1474560
  13.1 17.2 %collective-permute-start = (bf16[8,8,576]{2,1,0:T(8,128)(2,1)}, bf16[8,8,576]{2,1,0:T(8,128)(2,1)S(1)}, u32[]{:S(2)}, u32[]{:S(2)}) collective-permute-start(bf16[8,8,576]{2,1,0:T(8,128)(2,1)} %copy.187), channel_id=1, source_target_pairs={{120,0},{0,8},{8,16},{16,24},{24,32},{32,40},{40,48},{48,56},{56,6... | collective-permute-start | bytes 221192 | tf_op jit(solution)/shard_map/while/body/eval_jaxpr/ppermute | solution.py:13
  13.7 16.6 %collective-permute-start.1 = (bf16[8,8,512]{2,1,0:T(8,128)(2,1)}, bf16[8,8,512]{2,1,0:T(8,128)(2,1)S(1)}, u32[]{:S(2)}, u32[]{:S(2)}) collective-permute-start(bf16[8,8,512]{2,1,0:T(8,128)(2,1)} %copy.188), channel_id=1, source_target_pairs={{120,0},{0,8},{8,16},{16,24},{24,32},{32,40},{40,48},{48,56},{56,6... | collective-permute-start | bytes 196616 | tf_op jit(solution)/shard_map/while/body/eval_jaxpr/ppermute | solution.py:13
  30.9 14.6 %collective-permute-start = (bf16[8,8,576]{2,1,0:T(8,128)(2,1)}, bf16[8,8,576]{2,1,0:T(8,128)(2,1)S(1)}, u32[]{:S(2)}, u32[]{:S(2)}) collective-permute-start(bf16[8,8,576]{2,1,0:T(8,128)(2,1)} %copy.187), channel_id=1, source_target_pairs={{120,0},{0,8},{8,16},{16,24},{24,32},{32,40},{40,48},{48,56},{56,6... | collective-permute-start | bytes 221192 | tf_op jit(solution)/shard_map/while/body/eval_jaxpr/ppermute | solution.py:13
  31.6 14.0 %collective-permute-start.1 = (bf16[8,8,512]{2,1,0:T(8,128)(2,1)}, bf16[8,8,512]{2,1,0:T(8,128)(2,1)S(1)}, u32[]{:S(2)}, u32[]{:S(2)}) collective-permute-start(bf16[8,8,512]{2,1,0:T(8,128)(2,1)} %copy.188), channel_id=1, source_target_pairs={{120,0},{0,8},{8,16},{16,24},{24,32},{32,40},{40,48},{48,56},{56,6... | collective-permute-start | bytes 196616 | tf_op jit(solution)/shard_map/while/body/eval_jaxpr/ppermute | solution.py:13
  46.2 12.7 %collective-permute-start = (bf16[8,8,576]{2,1,0:T(8,128)(2,1)}, bf16[8,8,576]{2,1,0:T(8,128)(2,1)S(1)}, u32[]{:S(2)}, u32[]{:S(2)}) collective-permute-start(bf16[8,8,576]{2,1,0:T(8,128)(2,1)} %copy.187), channel_id=1, source_target_pairs={{120,0},{0,8},{8,16},{16,24},{24,32},{32,40},{40,48},{48,56},{56,6... | collective-permute-start | bytes 221192 | tf_op jit(solution)/shard_map/while/body/eval_jaxpr/ppermute | solution.py:13
  46.8 12.1 %collective-permute-start.1 = (bf16[8,8,512]{2,1,0:T(8,128)(2,1)}, bf16[8,8,512]{2,1,0:T(8,128)(2,1)S(1)}, u32[]{:S(2)}, u32[]{:S(2)}) collective-permute-start(bf16[8,8,512]{2,1,0:T(8,128)(2,1)} %copy.188), channel_id=1, source_target_pairs={{120,0},{0,8},{8,16},{16,24},{24,32},{32,40},{40,48},{48,56},{56,6... | collective-permute-start | bytes 196616 | tf_op jit(solution)/shard_map/while/body/eval_jaxpr/ppermute | solution.py:13
  59.6 12.7 %collective-permute-start = (bf16[8,8,576]{2,1,0:T(8,128)(2,1)}, bf16[8,8,576]{2,1,0:T(8,128)(2,1)S(1)}, u32[]{:S(2)}, u32[]{:S(2)}) collective-permute-start(bf16[8,8,576]{2,1,0:T(8,128)(2,1)} %copy.187), channel_id=1, source_target_pairs={{120,0},{0,8},{8,16},{16,24},{24,32},{32,40},{40,48},{48,56},{56,6... | collective-permute-start | bytes 221192 | tf_op jit(solution)/shard_map/while/body/eval_jaxpr/ppermute | solution.py:13
  60.2 12.1 %collective-permute-start.1 = (bf16[8,8,512]{2,1,0:T(8,128)(2,1)}, bf16[8,8,512]{2,1,0:T(8,128)(2,1)S(1)}, u32[]{:S(2)}, u32[]{:S(2)}) collective-permute-start(bf16[8,8,512]{2,1,0:T(8,128)(2,1)} %copy.188), channel_id=1, source_target_pairs={{120,0},{0,8},{8,16},{16,24},{24,32},{32,40},{40,48},{48,56},{56,6... | collective-permute-start | bytes 196616 | tf_op jit(solution)/shard_map/while/body/eval_jaxpr/ppermute | solution.py:13
  73.0 12.7 %collective-permute-start = (bf16[8,8,576]{2,1,0:T(8,128)(2,1)}, bf16[8,8,576]{2,1,0:T(8,128)(2,1)S(1)}, u32[]{:S(2)}, u32[]{:S(2)}) collective-permute-start(bf16[8,8,576]{2,1,0:T(8,128)(2,1)} %copy.187), channel_id=1, source_target_pairs={{120,0},{0,8},{8,16},{16,24},{24,32},{32,40},{40,48},{48,56},{56,6... | collective-permute-start | bytes 221192 | tf_op jit(solution)/shard_map/while/body/eval_jaxpr/ppermute | solution.py:13
  73.6 12.1 %collective-permute-start.1 = (bf16[8,8,512]{2,1,0:T(8,128)(2,1)}, bf16[8,8,512]{2,1,0:T(8,128)(2,1)S(1)}, u32[]{:S(2)}, u32[]{:S(2)}) collective-permute-start(bf16[8,8,512]{2,1,0:T(8,128)(2,1)} %copy.188), channel_id=1, source_target_pairs={{120,0},{0,8},{8,16},{16,24},{24,32},{32,40},{40,48},{48,56},{56,6... | collective-permute-start | bytes 196616 | tf_op jit(solution)/shard_map/while/body/eval_jaxpr/ppermute | solution.py:13
  86.4 12.7 %collective-permute-start = (bf16[8,8,576]{2,1,0:T(8,128)(2,1)}, bf16[8,8,576]{2,1,0:T(8,128)(2,1)S(1)}, u32[]{:S(2)}, u32[]{:S(2)}) collective-permute-start(bf16[8,8,576]{2,1,0:T(8,128)(2,1)} %copy.187), channel_id=1, source_target_pairs={{120,0},{0,8},{8,16},{16,24},{24,32},{32,40},{40,48},{48,56},{56,6... | collective-permute-start | bytes 221192 | tf_op jit(solution)/shard_map/while/body/eval_jaxpr/ppermute | solution.py:13
  87.0 12.1 %collective-permute-start.1 = (bf16[8,8,512]{2,1,0:T(8,128)(2,1)}, bf16[8,8,512]{2,1,0:T(8,128)(2,1)S(1)}, u32[]{:S(2)}, u32[]{:S(2)}) collective-permute-start(bf16[8,8,512]{2,1,0:T(8,128)(2,1)} %copy.188), channel_id=1, source_target_pairs={{120,0},{0,8},{8,16},{16,24},{24,32},{32,40},{40,48},{48,56},{56,6... | collective-permute-start | bytes 196616 | tf_op jit(solution)/shard_map/while/body/eval_jaxpr/ppermute | solution.py:13
  99.8 12.7 %collective-permute-start = (bf16[8,8,576]{2,1,0:T(8,128)(2,1)}, bf16[8,8,576]{2,1,0:T(8,128)(2,1)S(1)}, u32[]{:S(2)}, u32[]{:S(2)}) collective-permute-start(bf16[8,8,576]{2,1,0:T(8,128)(2,1)} %copy.187), channel_id=1, source_target_pairs={{120,0},{0,8},{8,16},{16,24},{24,32},{32,40},{40,48},{48,56},{56,6... | collective-permute-start | bytes 221192 | tf_op jit(solution)/shard_map/while/body/eval_jaxpr/ppermute | solution.py:13
  100.4 12.1 %collective-permute-start.1 = (bf16[8,8,512]{2,1,0:T(8,128)(2,1)}, bf16[8,8,512]{2,1,0:T(8,128)(2,1)S(1)}, u32[]{:S(2)}, u32[]{:S(2)}) collective-permute-start(bf16[8,8,512]{2,1,0:T(8,128)(2,1)} %copy.188), channel_id=1, source_target_pairs={{120,0},{0,8},{8,16},{16,24},{24,32},{32,40},{40,48},{48,56},{56,6... | collective-permute-start | bytes 196616 | tf_op jit(solution)/shard_map/while/body/eval_jaxpr/ppermute | solution.py:13
  113.2 12.7 %collective-permute-start = (bf16[8,8,576]{2,1,0:T(8,128)(2,1)}, bf16[8,8,576]{2,1,0:T(8,128)(2,1)S(1)}, u32[]{:S(2)}, u32[]{:S(2)}) collective-permute-start(bf16[8,8,576]{2,1,0:T(8,128)(2,1)} %copy.187), channel_id=1, source_target_pairs={{120,0},{0,8},{8,16},{16,24},{24,32},{32,40},{40,48},{48,56},{56,6... | collective-permute-start | bytes 221192 | tf_op jit(solution)/shard_map/while/body/eval_jaxpr/ppermute | solution.py:13
  113.8 12.1 %collective-permute-start.1 = (bf16[8,8,512]{2,1,0:T(8,128)(2,1)}, bf16[8,8,512]{2,1,0:T(8,128)(2,1)S(1)}, u32[]{:S(2)}, u32[]{:S(2)}) collective-permute-start(bf16[8,8,512]{2,1,0:T(8,128)(2,1)} %copy.188), channel_id=1, source_target_pairs={{120,0},{0,8},{8,16},{16,24},{24,32},{32,40},{40,48},{48,56},{56,6... | collective-permute-start | bytes 196616 | tf_op jit(solution)/shard_map/while/body/eval_jaxpr/ppermute | solution.py:13
  126.6 16.2 %collective-permute-start = (bf16[8,8,576]{2,1,0:T(8,128)(2,1)}, bf16[8,8,576]{2,1,0:T(8,128)(2,1)S(1)}, u32[]{:S(2)}, u32[]{:S(2)}) collective-permute-start(bf16[8,8,576]{2,1,0:T(8,128)(2,1)} %copy.187), channel_id=1, source_target_pairs={{120,0},{0,8},{8,16},{16,24},{24,32},{32,40},{40,48},{48,56},{56,6... | collective-permute-start | bytes 221192 | tf_op jit(solution)/shard_map/while/body/eval_jaxpr/ppermute | solution.py:13
  127.3 15.6 %collective-permute-start.1 = (bf16[8,8,512]{2,1,0:T(8,128)(2,1)}, bf16[8,8,512]{2,1,0:T(8,128)(2,1)S(1)}, u32[]{:S(2)}, u32[]{:S(2)}) collective-permute-start(bf16[8,8,512]{2,1,0:T(8,128)(2,1)} %copy.188), channel_id=1, source_target_pairs={{120,0},{0,8},{8,16},{16,24},{24,32},{32,40},{40,48},{48,56},{56,6... | collective-permute-start | bytes 196616 | tf_op jit(solution)/shard_map/while/body/eval_jaxpr/ppermute | solution.py:13
  132.4 10.4 %collective-permute-start.2 = (f32[8,8]{0,1:T(8,128)}, f32[8,8]{0,1:T(8,128)S(1)}, u32[]{:S(2)}, u32[]{:S(2)}) collective-permute-start(f32[8,8]{0,1:T(8,128)} %get-tuple-element.1096), channel_id=1, source_target_pairs={{120,0},{0,8},{8,16},{16,24},{24,32},{32,40},{40,48},{48,56},{56,6... | collective-permute-start | bytes 776 | tf_op jit(solution)/shard_map/while/body/eval_jaxpr/ppermute | solution.py:13
  143.5 12.7 %collective-permute-start = (bf16[8,8,576]{2,1,0:T(8,128)(2,1)}, bf16[8,8,576]{2,1,0:T(8,128)(2,1)S(1)}, u32[]{:S(2)}, u32[]{:S(2)}) collective-permute-start(bf16[8,8,576]{2,1,0:T(8,128)(2,1)} %copy.187), channel_id=1, source_target_pairs={{120,0},{0,8},{8,16},{16,24},{24,32},{32,40},{40,48},{48,56},{56,6... | collective-permute-start | bytes 221192 | tf_op jit(solution)/shard_map/while/body/eval_jaxpr/ppermute | solution.py:13
  144.1 12.1 %collective-permute-start.1 = (bf16[8,8,512]{2,1,0:T(8,128)(2,1)}, bf16[8,8,512]{2,1,0:T(8,128)(2,1)S(1)}, u32[]{:S(2)}, u32[]{:S(2)}) collective-permute-start(bf16[8,8,512]{2,1,0:T(8,128)(2,1)} %copy.188), channel_id=1, source_target_pairs={{120,0},{0,8},{8,16},{16,24},{24,32},{32,40},{40,48},{48,56},{56,6... | collective-permute-start | bytes 196616 | tf_op jit(solution)/shard_map/while/body/eval_jaxpr/ppermute | solution.py:13
  156.9 12.7 %collective-permute-start = (bf16[8,8,576]{2,1,0:T(8,128)(2,1)}, bf16[8,8,576]{2,1,0:T(8,128)(2,1)S(1)}, u32[]{:S(2)}, u32[]{:S(2)}) collective-permute-start(bf16[8,8,576]{2,1,0:T(8,128)(2,1)} %copy.187), channel_id=1, source_target_pairs={{120,0},{0,8},{8,16},{16,24},{24,32},{32,40},{40,48},{48,56},{56,6... | collective-permute-start | bytes 221192 | tf_op jit(solution)/shard_map/while/body/eval_jaxpr/ppermute | solution.py:13
  157.5 12.1 %collective-permute-start.1 = (bf16[8,8,512]{2,1,0:T(8,128)(2,1)}, bf16[8,8,512]{2,1,0:T(8,128)(2,1)S(1)}, u32[]{:S(2)}, u32[]{:S(2)}) collective-permute-start(bf16[8,8,512]{2,1,0:T(8,128)(2,1)} %copy.188), channel_id=1, source_target_pairs={{120,0},{0,8},{8,16},{16,24},{24,32},{32,40},{40,48},{48,56},{56,6... | collective-permute-start | bytes 196616 | tf_op jit(solution)/shard_map/while/body/eval_jaxpr/ppermute | solution.py:13
  170.3 14.3 %collective-permute-start = (bf16[8,8,576]{2,1,0:T(8,128)(2,1)}, bf16[8,8,576]{2,1,0:T(8,128)(2,1)S(1)}, u32[]{:S(2)}, u32[]{:S(2)}) collective-permute-start(bf16[8,8,576]{2,1,0:T(8,128)(2,1)} %copy.187), channel_id=1, source_target_pairs={{120,0},{0,8},{8,16},{16,24},{24,32},{32,40},{40,48},{48,56},{56,6... | collective-permute-start | bytes 221192 | tf_op jit(solution)/shard_map/while/body/eval_jaxpr/ppermute | solution.py:13
  170.9 13.6 %collective-permute-start.1 = (bf16[8,8,512]{2,1,0:T(8,128)(2,1)}, bf16[8,8,512]{2,1,0:T(8,128)(2,1)S(1)}, u32[]{:S(2)}, u32[]{:S(2)}) collective-permute-start(bf16[8,8,512]{2,1,0:T(8,128)(2,1)} %copy.188), channel_id=1, source_target_pairs={{120,0},{0,8},{8,16},{16,24},{24,32},{32,40},{40,48},{48,56},{56,6... | collective-permute-start | bytes 196616 | tf_op jit(solution)/shard_map/while/body/eval_jaxpr/ppermute | solution.py:13
  185.2 14.7 %collective-permute-start = (bf16[8,8,576]{2,1,0:T(8,128)(2,1)}, bf16[8,8,576]{2,1,0:T(8,128)(2,1)S(1)}, u32[]{:S(2)}, u32[]{:S(2)}) collective-permute-start(bf16[8,8,576]{2,1,0:T(8,128)(2,1)} %copy.187), channel_id=1, source_target_pairs={{120,0},{0,8},{8,16},{16,24},{24,32},{32,40},{40,48},{48,56},{56,6... | collective-permute-start | bytes 221192 | tf_op jit(solution)/shard_map/while/body/eval_jaxpr/ppermute | solution.py:13
  185.9 14.1 %collective-permute-start.1 = (bf16[8,8,512]{2,1,0:T(8,128)(2,1)}, bf16[8,8,512]{2,1,0:T(8,128)(2,1)S(1)}, u32[]{:S(2)}, u32[]{:S(2)}) collective-permute-start(bf16[8,8,512]{2,1,0:T(8,128)(2,1)} %copy.188), channel_id=1, source_target_pairs={{120,0},{0,8},{8,16},{16,24},{24,32},{32,40},{40,48},{48,56},{56,6... | collective-permute-start | bytes 196616 | tf_op jit(solution)/shard_map/while/body/eval_jaxpr/ppermute | solution.py:13
  200.6 17.3 %collective-permute-start = (bf16[8,8,576]{2,1,0:T(8,128)(2,1)}, bf16[8,8,576]{2,1,0:T(8,128)(2,1)S(1)}, u32[]{:S(2)}, u32[]{:S(2)}) collective-permute-start(bf16[8,8,576]{2,1,0:T(8,128)(2,1)} %copy.187), channel_id=1, source_target_pairs={{120,0},{0,8},{8,16},{16,24},{24,32},{32,40},{40,48},{48,56},{56,6... | collective-permute-start | bytes 221192 | tf_op jit(solution)/shard_map/while/body/eval_jaxpr/ppermute | solution.py:13
  201.2 16.6 %collective-permute-start.1 = (bf16[8,8,512]{2,1,0:T(8,128)(2,1)}, bf16[8,8,512]{2,1,0:T(8,128)(2,1)S(1)}, u32[]{:S(2)}, u32[]{:S(2)}) collective-permute-start(bf16[8,8,512]{2,1,0:T(8,128)(2,1)} %copy.188), channel_id=1, source_target_pairs={{120,0},{0,8},{8,16},{16,24},{24,32},{32,40},{40,48},{48,56},{56,6... | collective-permute-start | bytes 196616 | tf_op jit(solution)/shard_map/while/body/eval_jaxpr/ppermute | solution.py:13
  206.4 11.5 %collective-permute-start.2 = (f32[8,8]{0,1:T(8,128)}, f32[8,8]{0,1:T(8,128)S(1)}, u32[]{:S(2)}, u32[]{:S(2)}) collective-permute-start(f32[8,8]{0,1:T(8,128)} %get-tuple-element.1096), channel_id=1, source_target_pairs={{120,0},{0,8},{8,16},{16,24},{24,32},{32,40},{40,48},{48,56},{56,6... | collective-permute-start | bytes 776 | tf_op jit(solution)/shard_map/while/body/eval_jaxpr/ppermute | solution.py:13
  218.5 12.7 %collective-permute-start = (bf16[8,8,576]{2,1,0:T(8,128)(2,1)}, bf16[8,8,576]{2,1,0:T(8,128)(2,1)S(1)}, u32[]{:S(2)}, u32[]{:S(2)}) collective-permute-start(bf16[8,8,576]{2,1,0:T(8,128)(2,1)} %copy.187), channel_id=1, source_target_pairs={{120,0},{0,8},{8,16},{16,24},{24,32},{32,40},{40,48},{48,56},{56,6... | collective-permute-start | bytes 221192 | tf_op jit(solution)/shard_map/while/body/eval_jaxpr/ppermute | solution.py:13
  219.2 12.1 %collective-permute-start.1 = (bf16[8,8,512]{2,1,0:T(8,128)(2,1)}, bf16[8,8,512]{2,1,0:T(8,128)(2,1)S(1)}, u32[]{:S(2)}, u32[]{:S(2)}) collective-permute-start(bf16[8,8,512]{2,1,0:T(8,128)(2,1)} %copy.188), channel_id=1, source_target_pairs={{120,0},{0,8},{8,16},{16,24},{24,32},{32,40},{40,48},{48,56},{56,6... | collective-permute-start | bytes 196616 | tf_op jit(solution)/shard_map/while/body/eval_jaxpr/ppermute | solution.py:13
  250.0 10.0 %collective-permute-start.5 = (bf16[8,8,576]{2,1,0:T(8,128)(2,1)S(1)}, bf16[8,8,576]{2,1,0:T(8,128)(2,1)S(1)}, u32[]{:S(2)}, u32[]{:S(2)}) collective-permute-start(bf16[8,8,576]{2,1,0:T(8,128)(2,1)S(1)} %copy.212), channel_id=1, source_target_pairs={{120,0},{0,8},{8,16},{16,24},{24,32},{32,40},{40,48},{48,56},{56,6... | collective-permute-start | bytes 221192 | tf_op jit(solution)/shard_map/while/body/eval_jaxpr/ppermute | solution.py:13
  250.0 10.0 %collective-permute-start.6 = (bf16[8,8,512]{2,1,0:T(8,128)(2,1)S(1)}, bf16[8,8,512]{2,1,0:T(8,128)(2,1)}, u32[]{:S(2)}, u32[]{:S(2)}) collective-permute-start(bf16[8,8,512]{2,1,0:T(8,128)(2,1)S(1)} %copy.213), channel_id=1, source_target_pairs={{120,0},{0,8},{8,16},{16,24},{24,32},{32,40},{40,48},{48,56},{56,6... | collective-permute-start | bytes 196616 | tf_op jit(solution)/shard_map/while/body/eval_jaxpr/ppermute | solution.py:13
  265.3 10.0 %collective-permute-start.5 = (bf16[8,8,576]{2,1,0:T(8,128)(2,1)S(1)}, bf16[8,8,576]{2,1,0:T(8,128)(2,1)S(1)}, u32[]{:S(2)}, u32[]{:S(2)}) collective-permute-start(bf16[8,8,576]{2,1,0:T(8,128)(2,1)S(1)} %copy.212), channel_id=1, source_target_pairs={{120,0},{0,8},{8,16},{16,24},{24,32},{32,40},{40,48},{48,56},{56,6... | collective-permute-start | bytes 221192 | tf_op jit(solution)/shard_map/while/body/eval_jaxpr/ppermute | solution.py:13
  265.4 10.0 %collective-permute-start.6 = (bf16[8,8,512]{2,1,0:T(8,128)(2,1)S(1)}, bf16[8,8,512]{2,1,0:T(8,128)(2,1)}, u32[]{:S(2)}, u32[]{:S(2)}) collective-permute-start(bf16[8,8,512]{2,1,0:T(8,128)(2,1)S(1)} %copy.213), channel_id=1, source_target_pairs={{120,0},{0,8},{8,16},{16,24},{24,32},{32,40},{40,48},{48,56},{56,6... | collective-permute-start | bytes 196616 | tf_op jit(solution)/shard_map/while/body/eval_jaxpr/ppermute | solution.py:13
  280.7 10.0 %collective-permute-start.5 = (bf16[8,8,576]{2,1,0:T(8,128)(2,1)S(1)}, bf16[8,8,576]{2,1,0:T(8,128)(2,1)S(1)}, u32[]{:S(2)}, u32[]{:S(2)}) collective-permute-start(bf16[8,8,576]{2,1,0:T(8,128)(2,1)S(1)} %copy.212), channel_id=1, source_target_pairs={{120,0},{0,8},{8,16},{16,24},{24,32},{32,40},{40,48},{48,56},{56,6... | collective-permute-start | bytes 221192 | tf_op jit(solution)/shard_map/while/body/eval_jaxpr/ppermute | solution.py:13
  280.8 10.0 %collective-permute-start.6 = (bf16[8,8,512]{2,1,0:T(8,128)(2,1)S(1)}, bf16[8,8,512]{2,1,0:T(8,128)(2,1)}, u32[]{:S(2)}, u32[]{:S(2)}) collective-permute-start(bf16[8,8,512]{2,1,0:T(8,128)(2,1)S(1)} %copy.213), channel_id=1, source_target_pairs={{120,0},{0,8},{8,16},{16,24},{24,32},{32,40},{40,48},{48,56},{56,6... | collective-permute-start | bytes 196616 | tf_op jit(solution)/shard_map/while/body/eval_jaxpr/ppermute | solution.py:13
  296.1 10.0 %collective-permute-start.5 = (bf16[8,8,576]{2,1,0:T(8,128)(2,1)S(1)}, bf16[8,8,576]{2,1,0:T(8,128)(2,1)S(1)}, u32[]{:S(2)}, u32[]{:S(2)}) collective-permute-start(bf16[8,8,576]{2,1,0:T(8,128)(2,1)S(1)} %copy.212), channel_id=1, source_target_pairs={{120,0},{0,8},{8,16},{16,24},{24,32},{32,40},{40,48},{48,56},{56,6... | collective-permute-start | bytes 221192 | tf_op jit(solution)/shard_map/while/body/eval_jaxpr/ppermute | solution.py:13
  296.2 10.0 %collective-permute-start.6 = (bf16[8,8,512]{2,1,0:T(8,128)(2,1)S(1)}, bf16[8,8,512]{2,1,0:T(8,128)(2,1)}, u32[]{:S(2)}, u32[]{:S(2)}) collective-permute-start(bf16[8,8,512]{2,1,0:T(8,128)(2,1)S(1)} %copy.213), channel_id=1, source_target_pairs={{120,0},{0,8},{8,16},{16,24},{24,32},{32,40},{40,48},{48,56},{56,6... | collective-permute-start | bytes 196616 | tf_op jit(solution)/shard_map/while/body/eval_jaxpr/ppermute | solution.py:13
  311.5 10.0 %collective-permute-start.5 = (bf16[8,8,576]{2,1,0:T(8,128)(2,1)S(1)}, bf16[8,8,576]{2,1,0:T(8,128)(2,1)S(1)}, u32[]{:S(2)}, u32[]{:S(2)}) collective-permute-start(bf16[8,8,576]{2,1,0:T(8,128)(2,1)S(1)} %copy.212), channel_id=1, source_target_pairs={{120,0},{0,8},{8,16},{16,24},{24,32},{32,40},{40,48},{48,56},{56,6... | collective-permute-start | bytes 221192 | tf_op jit(solution)/shard_map/while/body/eval_jaxpr/ppermute | solution.py:13
  311.6 10.0 %collective-permute-start.6 = (bf16[8,8,512]{2,1,0:T(8,128)(2,1)S(1)}, bf16[8,8,512]{2,1,0:T(8,128)(2,1)}, u32[]{:S(2)}, u32[]{:S(2)}) collective-permute-start(bf16[8,8,512]{2,1,0:T(8,128)(2,1)S(1)} %copy.213), channel_id=1, source_target_pairs={{120,0},{0,8},{8,16},{16,24},{24,32},{32,40},{40,48},{48,56},{56,6... | collective-permute-start | bytes 196616 | tf_op jit(solution)/shard_map/while/body/eval_jaxpr/ppermute | solution.py:13
  326.9 10.0 %collective-permute-start.5 = (bf16[8,8,576]{2,1,0:T(8,128)(2,1)S(1)}, bf16[8,8,576]{2,1,0:T(8,128)(2,1)S(1)}, u32[]{:S(2)}, u32[]{:S(2)}) collective-permute-start(bf16[8,8,576]{2,1,0:T(8,128)(2,1)S(1)} %copy.212), channel_id=1, source_target_pairs={{120,0},{0,8},{8,16},{16,24},{24,32},{32,40},{40,48},{48,56},{56,6... | collective-permute-start | bytes 221192 | tf_op jit(solution)/shard_map/while/body/eval_jaxpr/ppermute | solution.py:13
  326.9 10.0 %collective-permute-start.6 = (bf16[8,8,512]{2,1,0:T(8,128)(2,1)S(1)}, bf16[8,8,512]{2,1,0:T(8,128)(2,1)}, u32[]{:S(2)}, u32[]{:S(2)}) collective-permute-start(bf16[8,8,512]{2,1,0:T(8,128)(2,1)S(1)} %copy.213), channel_id=1, source_target_pairs={{120,0},{0,8},{8,16},{16,24},{24,32},{32,40},{40,48},{48,56},{56,6... | collective-permute-start | bytes 196616 | tf_op jit(solution)/shard_map/while/body/eval_jaxpr/ppermute | solution.py:13
  342.2 10.0 %collective-permute-start.5 = (bf16[8,8,576]{2,1,0:T(8,128)(2,1)S(1)}, bf16[8,8,576]{2,1,0:T(8,128)(2,1)S(1)}, u32[]{:S(2)}, u32[]{:S(2)}) collective-permute-start(bf16[8,8,576]{2,1,0:T(8,128)(2,1)S(1)} %copy.212), channel_id=1, source_target_pairs={{120,0},{0,8},{8,16},{16,24},{24,32},{32,40},{40,48},{48,56},{56,6... | collective-permute-start | bytes 221192 | tf_op jit(solution)/shard_map/while/body/eval_jaxpr/ppermute | solution.py:13
  342.3 10.0 %collective-permute-start.6 = (bf16[8,8,512]{2,1,0:T(8,128)(2,1)S(1)}, bf16[8,8,512]{2,1,0:T(8,128)(2,1)}, u32[]{:S(2)}, u32[]{:S(2)}) collective-permute-start(bf16[8,8,512]{2,1,0:T(8,128)(2,1)S(1)} %copy.213), channel_id=1, source_target_pairs={{120,0},{0,8},{8,16},{16,24},{24,32},{32,40},{40,48},{48,56},{56,6... | collective-permute-start | bytes 196616 | tf_op jit(solution)/shard_map/while/body/eval_jaxpr/ppermute | solution.py:13
  357.6 10.0 %collective-permute-start.5 = (bf16[8,8,576]{2,1,0:T(8,128)(2,1)S(1)}, bf16[8,8,576]{2,1,0:T(8,128)(2,1)S(1)}, u32[]{:S(2)}, u32[]{:S(2)}) collective-permute-start(bf16[8,8,576]{2,1,0:T(8,128)(2,1)S(1)} %copy.212), channel_id=1, source_target_pairs={{120,0},{0,8},{8,16},{16,24},{24,32},{32,40},{40,48},{48,56},{56,6... | collective-permute-start | bytes 221192 | tf_op jit(solution)/shard_map/while/body/eval_jaxpr/ppermute | solution.py:13
  357.7 10.0 %collective-permute-start.6 = (bf16[8,8,512]{2,1,0:T(8,128)(2,1)S(1)}, bf16[8,8,512]{2,1,0:T(8,128)(2,1)}, u32[]{:S(2)}, u32[]{:S(2)}) collective-permute-start(bf16[8,8,512]{2,1,0:T(8,128)(2,1)S(1)} %copy.213), channel_id=1, source_target_pairs={{120,0},{0,8},{8,16},{16,24},{24,32},{32,40},{40,48},{48,56},{56,6... | collective-permute-start | bytes 196616 | tf_op jit(solution)/shard_map/while/body/eval_jaxpr/ppermute | solution.py:13
  373.0 10.0 %collective-permute-start.5 = (bf16[8,8,576]{2,1,0:T(8,128)(2,1)S(1)}, bf16[8,8,576]{2,1,0:T(8,128)(2,1)S(1)}, u32[]{:S(2)}, u32[]{:S(2)}) collective-permute-start(bf16[8,8,576]{2,1,0:T(8,128)(2,1)S(1)} %copy.212), channel_id=1, source_target_pairs={{120,0},{0,8},{8,16},{16,24},{24,32},{32,40},{40,48},{48,56},{56,6... | collective-permute-start | bytes 221192 | tf_op jit(solution)/shard_map/while/body/eval_jaxpr/ppermute | solution.py:13
  373.1 10.0 %collective-permute-start.6 = (bf16[8,8,512]{2,1,0:T(8,128)(2,1)S(1)}, bf16[8,8,512]{2,1,0:T(8,128)(2,1)}, u32[]{:S(2)}, u32[]{:S(2)}) collective-permute-start(bf16[8,8,512]{2,1,0:T(8,128)(2,1)S(1)} %copy.213), channel_id=1, source_target_pairs={{120,0},{0,8},{8,16},{16,24},{24,32},{32,40},{40,48},{48,56},{56,6... | collective-permute-start | bytes 196616 | tf_op jit(solution)/shard_map/while/body/eval_jaxpr/ppermute | solution.py:13
  388.4 10.0 %collective-permute-start.5 = (bf16[8,8,576]{2,1,0:T(8,128)(2,1)S(1)}, bf16[8,8,576]{2,1,0:T(8,128)(2,1)S(1)}, u32[]{:S(2)}, u32[]{:S(2)}) collective-permute-start(bf16[8,8,576]{2,1,0:T(8,128)(2,1)S(1)} %copy.212), channel_id=1, source_target_pairs={{120,0},{0,8},{8,16},{16,24},{24,32},{32,40},{40,48},{48,56},{56,6... | collective-permute-start | bytes 221192 | tf_op jit(solution)/shard_map/while/body/eval_jaxpr/ppermute | solution.py:13
  388.4 10.0 %collective-permute-start.6 = (bf16[8,8,512]{2,1,0:T(8,128)(2,1)S(1)}, bf16[8,8,512]{2,1,0:T(8,128)(2,1)}, u32[]{:S(2)}, u32[]{:S(2)}) collective-permute-start(bf16[8,8,512]{2,1,0:T(8,128)(2,1)S(1)} %copy.213), channel_id=1, source_target_pairs={{120,0},{0,8},{8,16},{16,24},{24,32},{32,40},{40,48},{48,56},{56,6... | collective-permute-start | bytes 196616 | tf_op jit(solution)/shard_map/while/body/eval_jaxpr/ppermute | solution.py:13
  403.7 10.0 %collective-permute-start.5 = (bf16[8,8,576]{2,1,0:T(8,128)(2,1)S(1)}, bf16[8,8,576]{2,1,0:T(8,128)(2,1)S(1)}, u32[]{:S(2)}, u32[]{:S(2)}) collective-permute-start(bf16[8,8,576]{2,1,0:T(8,128)(2,1)S(1)} %copy.212), channel_id=1, source_target_pairs={{120,0},{0,8},{8,16},{16,24},{24,32},{32,40},{40,48},{48,56},{56,6... | collective-permute-start | bytes 221192 | tf_op jit(solution)/shard_map/while/body/eval_jaxpr/ppermute | solution.py:13
  403.8 10.0 %collective-permute-start.6 = (bf16[8,8,512]{2,1,0:T(8,128)(2,1)S(1)}, bf16[8,8,512]{2,1,0:T(8,128)(2,1)}, u32[]{:S(2)}, u32[]{:S(2)}) collective-permute-start(bf16[8,8,512]{2,1,0:T(8,128)(2,1)S(1)} %copy.213), channel_id=1, source_target_pairs={{120,0},{0,8},{8,16},{16,24},{24,32},{32,40},{40,48},{48,56},{56,6... | collective-permute-start | bytes 196616 | tf_op jit(solution)/shard_map/while/body/eval_jaxpr/ppermute | solution.py:13
  419.1 10.0 %collective-permute-start.5 = (bf16[8,8,576]{2,1,0:T(8,128)(2,1)S(1)}, bf16[8,8,576]{2,1,0:T(8,128)(2,1)S(1)}, u32[]{:S(2)}, u32[]{:S(2)}) collective-permute-start(bf16[8,8,576]{2,1,0:T(8,128)(2,1)S(1)} %copy.212), channel_id=1, source_target_pairs={{120,0},{0,8},{8,16},{16,24},{24,32},{32,40},{40,48},{48,56},{56,6... | collective-permute-start | bytes 221192 | tf_op jit(solution)/shard_map/while/body/eval_jaxpr/ppermute | solution.py:13
  419.2 10.0 %collective-permute-start.6 = (bf16[8,8,512]{2,1,0:T(8,128)(2,1)S(1)}, bf16[8,8,512]{2,1,0:T(8,128)(2,1)}, u32[]{:S(2)}, u32[]{:S(2)}) collective-permute-start(bf16[8,8,512]{2,1,0:T(8,128)(2,1)S(1)} %copy.213), channel_id=1, source_target_pairs={{120,0},{0,8},{8,16},{16,24},{24,32},{32,40},{40,48},{48,56},{56,6... | collective-permute-start | bytes 196616 | tf_op jit(solution)/shard_map/while/body/eval_jaxpr/ppermute | solution.py:13
  434.5 10.0 %collective-permute-start.5 = (bf16[8,8,576]{2,1,0:T(8,128)(2,1)S(1)}, bf16[8,8,576]{2,1,0:T(8,128)(2,1)S(1)}, u32[]{:S(2)}, u32[]{:S(2)}) collective-permute-start(bf16[8,8,576]{2,1,0:T(8,128)(2,1)S(1)} %copy.212), channel_id=1, source_target_pairs={{120,0},{0,8},{8,16},{16,24},{24,32},{32,40},{40,48},{48,56},{56,6... | collective-permute-start | bytes 221192 | tf_op jit(solution)/shard_map/while/body/eval_jaxpr/ppermute | solution.py:13
  449.9 10.0 %collective-permute-start.5 = (bf16[8,8,576]{2,1,0:T(8,128)(2,1)S(1)}, bf16[8,8,576]{2,1,0:T(8,128)(2,1)S(1)}, u32[]{:S(2)}, u32[]{:S(2)}) collective-permute-start(bf16[8,8,576]{2,1,0:T(8,128)(2,1)S(1)} %copy.212), channel_id=1, source_target_pairs={{120,0},{0,8},{8,16},{16,24},{24,32},{32,40},{40,48},{48,56},{56,6... | collective-permute-start | bytes 221192 | tf_op jit(solution)/shard_map/while/body/eval_jaxpr/ppermute | solution.py:13
  465.2 10.0 %collective-permute-start.5 = (bf16[8,8,576]{2,1,0:T(8,128)(2,1)S(1)}, bf16[8,8,576]{2,1,0:T(8,128)(2,1)S(1)}, u32[]{:S(2)}, u32[]{:S(2)}) collective-permute-start(bf16[8,8,576]{2,1,0:T(8,128)(2,1)S(1)} %copy.212), channel_id=1, source_target_pairs={{120,0},{0,8},{8,16},{16,24},{24,32},{32,40},{40,48},{48,56},{56,6... | collective-permute-start | bytes 221192 | tf_op jit(solution)/shard_map/while/body/eval_jaxpr/ppermute | solution.py:13
  492.0 46.0 %all-to-all-start = ((bf16[8,1,64]{2,1,0:T(2,128)(2,1)}), bf16[8,1,64]{2,1,0:T(2,128)(2,1)S(1)}, u32[]{:S(2)}, u32[]{:S(2)}) async-start(bf16[8,1,64]{2,1,0:T(2,128)(2,1)} %all_to_all.20), calls=%async_computation | async-start | bytes 8192 | tf_op jit(solution)/shard_map/all_to_all | solution.py:226
  537.9 75.3 %all-to-all-start.1 = ((bf16[8,64,5120]{2,1,0:T(8,128)(2,1)}), bf16[8,64,5120]{2,1,0:T(8,128)(2,1)}, u32[]{:S(2)}, u32[]{:S(2)}) async-start(bf16[8,64,5120]{2,1,0:T(8,128)(2,1)} %bitcast.230), calls=%async_computation.1 | async-start | bytes 10485760 | tf_op jit(solution)/shard_map/all_to_all | solution.py:219
  542.6 189.2 %reduce-scatter.9.cloned.1.call-start = ((), (), s32[]{:S(2)}) async-start(), calls=%async_computation.6 | async-start | bytes 8355840
  655.4 13.6 %all-to-all-start.2 = ((f32[8,1,64]{2,1,0:T(1,128)}), f32[8,1,64]{2,1,0:T(1,128)S(1)}, u32[]{:S(2)}, u32[]{:S(2)}) async-start(f32[8,1,64]{2,1,0:T(1,128)} %all_to_all.18), calls=%async_computation.2 | async-start | bytes 8192 | tf_op jit(solution)/shard_map/all_to_all | solution.py:246
  (125 other events, 1974.4 us)
Sparse Core Ops, SparseCore 0:
  489.5 39.1 reduce-scatter.6
  637.1 94.7 reduce-scatter.8
where the time goes:
time: 746 us; the launch traced here: 742 us
  waiting for transfers between devices  407 us (55%)
  matrix products  149 us (20%)
  local copies, waits for them, and re-layouts  77.3 us (10%)
  other arithmetic  46.2 us (6%)
  starting transfers between devices  42.9 us (6%)
  between operations  14.4 us (2%)
    ppermute x154, waiting for transfers between devices, from_behind(): return lax.ppermute(block, axis, route)  244 us
    unnamed x4, waiting for transfers between devices  92.5 us
    all_to_all x1, waiting for transfers between devices, body(): lax.all_to_all(outgoing.reshape(expert_count, capacity, -1), 'exp', split...  70.6 us
    dot_general x32, matrix products, block_terms(): jnp.einsum('qhk,nk->hqn', query_heads, key_block, preferred_element_type=...  54.2 us
    while x135, local copies, waits for them, and re-layouts  45.6 us
    dot_general x32, matrix products, block_terms(): jnp.einsum('qhl,nl->hqn', grad_heads, key_block[:, :value_width], preferr...  30.5 us
    ppermute x154, starting transfers between devices, from_behind(): return lax.ppermute(block, axis, route)  29.8 us
    unnamed x33, local copies, waits for them, and re-layouts  23.6 us
  transfers between devices with their start and end apart: 159, of which 55 were waited for; matrix products, arithmetic and copies ran while one was open for 18% of the time, Pallas kernels for 0%

commit v1 on v0

v1 whole, which is shorter than its diff:
```python
import functools
import jax
import jax.numpy as jnp
from jax import lax
from jax.experimental import pallas as pl
from jax.experimental.pallas import tpu as pltpu
from jax.sharding import PartitionSpec as P

EPSILON = 1e-06
NEG_LARGE = -1e30
MESH = pl.DeviceIdType.MESH
F32 = jnp.float32
BF16 = jnp.bfloat16
LANES = 128


def padded(width):
    return -(-width // LANES) * LANES


def nt_dot(a, b):
    return lax.dot_general(a, b, (((1,), (1,)), ((), ())), preferred_element_type=F32)


def tn_dot(a, b):
    return lax.dot_general(a, b, (((0,), (0,)), ((), ())), preferred_element_type=F32)


def push(src, dst, send, recv, where):
    return pltpu.make_async_remote_copy(
        src_ref=src, dst_ref=dst, send_sem=send, recv_sem=recv, device_id=where, device_id_type=MESH
    )


def greet(axes):
    barrier = pltpu.get_barrier_semaphore()
    total = 0
    for axis, count in axes:
        me = lax.axis_index(axis)

        @pl.loop(0, count)
        def _(i):
            @pl.when(i != me)
            def _():
                pl.semaphore_signal(barrier, inc=1, device_id={axis: i}, device_id_type=MESH)

        total += count - 1
    pl.semaphore_wait(barrier, total)


def attention_kernel(
    sizes,
    rows_ref,
    key_ref,
    key_out,
    query_out,
    rows_all,
    stats_all,
    keys,
    weights,
    grads,
    score_grads,
    key_parts,
    key_all,
    query_parts,
    query_all,
    rows_send,
    rows_recv,
    stats_send,
    stats_recv,
    key_send,
    key_recv,
    query_send,
    query_recv,
):
    n_ctx, n_exp, key_width, value_width, query_rows, heads = sizes
    wide = padded(key_width)
    me = lax.axis_index("ctx")
    mine = lax.axis_index("exp")
    key_count = key_ref.shape[0]
    per = query_rows * heads
    scale = key_width ** (-0.5)
    group = 4
    cols = group * per
    n_groups = n_ctx // group
    tiles = cols // LANES

    greet((("ctx", n_ctx), ("exp", n_exp)))

    def rows_copy(there, source):
        return push(
            rows_ref, rows_all.at[source], rows_send.at[there], rows_recv.at[source], {"ctx": there}
        )

    @pl.loop(0, me)
    def _(i):
        rows_copy(me - 1 - i, me).start()

    @pl.loop(0, me)
    def _(i):
        rows_all[i] = jnp.zeros(rows_all.shape[1:], BF16)

    rows_all[me] = rows_ref[...]
    keys[:, :key_width] = key_ref[...]
    keys[:, key_width:] = jnp.zeros((key_count, wide - key_width), BF16)

    @pl.loop(0, n_groups)
    def _(g):
        for k in range(group):
            b = g * group + k

            @pl.when(b > me)
            def _():
                rows_copy(0, b).wait_recv()

        block = rows_all[pl.ds(g * group, group)].reshape(cols, rows_all.shape[2])
        at = pl.ds(pl.multiple_of(g * cols, cols), cols)
        scores = nt_dot(keys[...], block[:, :wide]) * scale
        prob_grads = nt_dot(keys[:, :value_width], block[:, wide:])
        column = lax.broadcasted_iota(jnp.int32, (1, cols), 1)
        last = (
            (g * group + column // per - me) * key_count
            + key_count
            - query_rows
            + (column % per) // heads
        )
        visible = lax.broadcasted_iota(jnp.int32, (key_count, cols), 0) <= last
        masked = jnp.where(visible, scores, NEG_LARGE)
        top = jnp.max(masked, axis=0, keepdims=True)
        grown = jnp.where(visible, jnp.exp(masked - top), 0.0)
        total = jnp.sum(grown, axis=0, keepdims=True)
        dotted = jnp.sum(grown * prob_grads, axis=0, keepdims=True)
        weights[:, at] = grown
        grads[:, at] = prob_grads
        for k in range(tiles):
            part = slice(k * LANES, (k + 1) * LANES)
            for n, value in enumerate((top, total, dotted)):
                stats_all[me, n, pl.ds(g * tiles + k, 1)] = value[:, part]

    def stats_copy(there, source):
        return push(
            stats_all.at[source],
            stats_all.at[source],
            stats_send.at[there],
            stats_recv.at[source],
            {"ctx": there},
        )

    @pl.loop(0, n_ctx)
    def _(i):
        @pl.when(i != me)
        def _():
            stats_copy(i, me).start()

    @pl.loop(0, n_ctx)
    def _(i):
        @pl.when(i != me)
        def _():
            stats_copy(me, i).wait_recv()

    tops = stats_all[:, 0]
    peak = jnp.max(tops, axis=0)
    factors = jnp.exp(tops - peak[None])
    total = jnp.sum(stats_all[:, 1] * factors, axis=0)
    delta = jnp.sum(stats_all[:, 2] * factors, axis=0) / total
    share = jnp.exp(stats_all[me, 0] - peak) / total
    share_row = jnp.concatenate([share[n : n + 1] for n in range(share.shape[0])], axis=1)
    delta_row = jnp.concatenate([delta[n : n + 1] for n in range(delta.shape[0])], axis=1)

    def key_copy(there, source):
        return push(
            key_parts.at[there], key_all.at[source], key_send.at[there], key_recv.at[source], {"exp": there}
        )

    piece = key_count // n_exp
    step = 2 * piece

    @pl.loop(0, key_count // step)
    def _(n):
        at = pl.ds(pl.multiple_of(n * step, step), step)
        probs = weights[at, :] * share_row
        now = (probs * (grads[at, :] - delta_row)).astype(BF16)
        score_grads[at, :] = now
        flat = rows_all[...].reshape(n_ctx * per, rows_all.shape[2])
        through = jnp.dot(now, flat[:, :wide], preferred_element_type=F32) * scale
        value = jnp.dot(probs.astype(BF16), flat[:, wide:], preferred_element_type=F32)
        for k in range(2):
            part = slice(k * piece, (k + 1) * piece)
            key_parts[2 * n + k, :, :value_width] = (
                through[part, :value_width] + value[part]
            ).astype(BF16)
            key_parts[2 * n + k, :, value_width:] = through[part, value_width:].astype(BF16)

            @pl.when(2 * n + k != mine)
            def _():
                key_copy(2 * n + k, mine).start()

    key_all[mine] = key_parts[mine]

    def query_copy(there, source):
        return push(
            query_parts.at[there],
            query_all.at[source],
            query_send.at[there],
            query_recv.at[source],
            {"ctx": there},
        )

    @pl.loop(0, n_groups)
    def _(g):
        at = pl.ds(pl.multiple_of(g * cols, cols), cols)
        part = tn_dot(score_grads[:, at], keys[...]) * scale
        query_parts[pl.ds(g * group, group)] = part.astype(BF16).reshape(group, per, wide)
        for k in range(group):
            b = g * group + k

            @pl.when(b > me)
            def _():
                query_copy(b, me).start()

    @pl.loop(0, n_exp)
    def _(s):
        @pl.when(s != mine)
        def _():
            key_copy(mine, s).wait_recv()

    key_total = key_all[0].astype(F32)
    for s in range(1, n_exp):
        key_total = key_total + key_all[s].astype(F32)
    key_out[...] = key_total.astype(BF16)

    def add(i, so_far):
        query_copy(me, i).wait_recv()
        return so_far + query_all[i].astype(F32)

    query_out[...] = lax.fori_loop(0, me, add, query_parts[me].astype(F32)).astype(BF16)

    @pl.loop(0, me)
    def _(i):
        rows_copy(i, me).wait_send()

    @pl.loop(0, n_ctx)
    def _(i):
        @pl.when(i != me)
        def _():
            stats_copy(i, me).wait_send()

        @pl.when(i > me)
        def _():
            query_copy(i, me).wait_send()

    @pl.loop(0, n_exp)
    def _(s):
        @pl.when(s != mine)
        def _():
            key_copy(s, mine).wait_send()


def attention(queries, latents, out_grad):
    key_count, key_width = latents.shape
    query_rows = queries.shape[0]
    heads = queries.shape[1] // key_width
    value_width = out_grad.shape[1] // heads
    per = query_rows * heads
    wide = padded(key_width)
    n_ctx, n_exp = lax.axis_size("ctx"), lax.axis_size("exp")
    piece = key_count // n_exp
    total_rows = n_ctx * per
    rows = jnp.concatenate(
        [
            queries.reshape(per, key_width),
            jnp.zeros((per, wide - key_width), BF16),
            out_grad.reshape(per, value_width),
        ],
        axis=1,
    )
    sizes = (n_ctx, n_exp, key_width, value_width, query_rows, heads)
    vmem = pl.BlockSpec(memory_space=pltpu.VMEM)
    dma = pltpu.SemaphoreType.DMA
    key_rows, query_grad = pl.pallas_call(
        functools.partial(attention_kernel, sizes),
        out_shape=(
            jax.ShapeDtypeStruct((piece, wide), BF16),
            jax.ShapeDtypeStruct((per, wide), BF16),
        ),
        in_specs=[vmem, vmem],
        out_specs=(vmem, vmem),
        scratch_shapes=[
            pltpu.VMEM((n_ctx, per, wide + value_width), BF16),
            pltpu.VMEM((n_ctx, 3, total_rows // LANES, LANES), F32),
            pltpu.VMEM((key_count, wide), BF16),
            pltpu.VMEM((key_count, total_rows), F32),
            pltpu.VMEM((key_count, total_rows), F32),
            pltpu.VMEM((key_count, total_rows), BF16),
            pltpu.VMEM((n_exp, piece, wide), BF16),
            pltpu.VMEM((n_exp, piece, wide), BF16),
            pltpu.VMEM((n_ctx, per, wide), BF16),
            pltpu.VMEM((n_ctx, per, wide), BF16),
            dma((n_ctx,)),
            dma((n_ctx,)),
            dma((n_ctx,)),
            dma((n_ctx,)),
            dma((n_exp,)),
            dma((n_exp,)),
            dma((n_ctx,)),
            dma((n_ctx,)),
        ],
        compiler_params=pltpu.CompilerParams(
            collective_id=0, has_side_effects=True, vmem_limit_bytes=56 * 2**20
        ),
    )(rows, latents)
    query_grad = query_grad[:, :key_width].reshape(query_rows, heads * key_width)
    return query_grad, key_rows[:, :key_width]


def body(
    queries,
    latents,
    out_grad,
    hidden_rows,
    norm_gain,
    latent_proj,
    stream_grad,
    expert_ids,
    route_weights,
    expert_acts,
    down_proj,
):
    query_grad, key_rows = attention(queries, latents, out_grad)
    norm_grad = lax.dot_general(
        key_rows, latent_proj, (((1,), (1,)), ((), ())), preferred_element_type=jnp.float32
    )
    row_values = hidden_rows.astype(jnp.float32)
    inverse = lax.rsqrt(jnp.mean(row_values * row_values, axis=-1, keepdims=True) + EPSILON)
    gained = norm_gain * norm_grad
    through_norm = inverse * gained - row_values * (inverse * inverse * inverse) * jnp.mean(
        row_values * gained, axis=-1, keepdims=True
    )
    stream_total = (stream_grad.astype(jnp.float32) + through_norm).astype(jnp.bfloat16)
    expert_count = lax.axis_size("exp")
    slot_count = expert_acts.shape[1]
    capacity = slot_count // expert_count
    local_rows = expert_ids.shape[0]
    top_count = expert_ids.shape[1]
    flat_ids = expert_ids.reshape(-1)
    chosen = (flat_ids[:, None] == jnp.arange(expert_count, dtype=jnp.int32)[None, :]).astype(
        jnp.int32
    )
    earlier = jnp.cumsum(chosen, axis=0) - chosen
    slot_of = flat_ids * capacity + jnp.sum(earlier * chosen, axis=1)
    select = (slot_of[:, None] == jnp.arange(slot_count, dtype=jnp.int32)[None, :]).astype(
        jnp.float32
    )
    select = select.reshape(local_rows, top_count, slot_count)
    placing = jnp.sum(select, axis=1).astype(jnp.bfloat16)
    outgoing = lax.dot_general(
        placing, stream_total, (((0,), (0,)), ((), ())), preferred_element_type=jnp.float32
    ).astype(jnp.bfloat16)
    rounded_weights = lax.optimization_barrier(route_weights.astype(jnp.bfloat16)).astype(
        jnp.float32
    )
    weight_slots = jnp.einsum("tks,tk->s", select, rounded_weights).astype(jnp.bfloat16)
    arrived, arrived_weights = (
        lax.all_to_all(
            outgoing.reshape(expert_count, capacity, -1),
            "exp",
            split_axis=0,
            concat_axis=0,
            tiled=True,
        ),
        lax.all_to_all(
            weight_slots.reshape(expert_count, capacity),
            "exp",
            split_axis=0,
            concat_axis=0,
            tiled=True,
        ),
    )
    arrived = arrived.reshape(slot_count, -1)
    arrived_weights = arrived_weights.reshape(slot_count)
    expert_rows = expert_acts[0]
    weight = down_proj[0]
    scaled = (arrived_weights.astype(jnp.float32)[:, None] * arrived.astype(jnp.float32)).astype(
        jnp.bfloat16
    )
    act_grad = lax.dot_general(
        scaled, weight, (((1,), (1,)), ((), ())), preferred_element_type=jnp.float32
    ).astype(jnp.bfloat16)
    outputs = jnp.dot(expert_rows, weight, preferred_element_type=jnp.float32)
    slot_grads = jnp.sum(arrived.astype(jnp.float32) * outputs, axis=1)
    returned = lax.all_to_all(
        slot_grads.reshape(expert_count, capacity), "exp", split_axis=0, concat_axis=0, tiled=True
    ).reshape(slot_count)
    weight_grad = jnp.einsum("tks,s->tk", select, returned)
    down_share = lax.psum_scatter(
        lax.dot_general(
            expert_rows, scaled, (((0,), (0,)), ((), ())), preferred_element_type=jnp.float32
        ).astype(jnp.bfloat16),
        "ctx",
        scatter_dimension=0,
        tiled=True,
    )
    return (query_grad, stream_total, act_grad[None], down_share[None], weight_grad)


def solution(mesh):
    in_specs = (
        P("ctx", "exp"),
        P("ctx", None),
        P("ctx", "exp"),
        P(("ctx", "exp"), None),
        P(),
        P(),
        P(("ctx", "exp"), None),
        P(("ctx", "exp"), None),
        P(("ctx", "exp"), None),
        P("exp", "ctx", None),
        P("exp", None, None),
    )
    out_specs = (
        P("ctx", "exp"),
        P(("ctx", "exp"), None),
        P("exp", "ctx", None),
        P("exp", "ctx", None),
        P(("ctx", "exp"), None),
    )
    return jax.shard_map(body, mesh=mesh, in_specs=in_specs, out_specs=out_specs, check_vma=False)
```

time: 746 us -> 319 us (0.43)
  waiting for transfers between devices: 407 us -> 149 us
  matrix products: 149 us -> 35.5 us
  Pallas kernels: 0 us -> 70 us
  local copies, waits for them, and re-layouts: 77.3 us -> 26.1 us
  other arithmetic: 46.2 us -> 7.88 us
  starting transfers between devices: 42.9 us -> 15.2 us
    ppermute x154 -> x0, waiting for transfers between devices: 244 us -> none  [from_behind(): return lax.ppermute(block, axis, route)]
    dot_general x112 -> x0, matrix products: 114 us -> none  [the longest x32 54.2 us: block_terms(): jnp.einsum('qhk,nk->hqn', query_heads, key_block, preferred_element_type=...]
    pallas_call x0 -> x1, Pallas kernels: none -> 70 us  [attention(): pl.pallas_call(functools.partial(attention_kernel, sizes), out_shape=(jax...]
    while x135 -> x0, local copies, waits for them, and re-layouts: 45.6 us -> none
    ppermute x154 -> x0, starting transfers between devices: 29.8 us -> none  [from_behind(): return lax.ppermute(block, axis, route)]
    unnamed x4 -> x2, waiting for transfers between devices: 92.5 us -> 75 us
    reduce_sum x16 -> x0, other arithmetic: 14.3 us -> none  [forward_update(): new_sum = running_sum * factor + jnp.sum(weights, axis=-1)]
    add x79 -> x0, other arithmetic: 11.3 us -> none  [the longest x16 11.1 us: forward_update(): new_dot = running_dot * factor + jnp.sum(weights * prob_grads, axis=-1)]
  transfers between devices with their start and end apart: 159 -> 4, of which waited for: 55 -> 2; matrix products, arithmetic and copies ran while one was open for 18% -> 12% of each run, Pallas kernels for 0% -> 22%
where the time goes in v1:
time: 319 us; the launch traced here: 318 us
  waiting for transfers between devices  149 us (47%)
  Pallas kernels  70 us (22%)
  matrix products  35.5 us (11%)
  local copies, waits for them, and re-layouts  26.1 us (8%)
  starting transfers between devices  15.2 us (5%)
  between operations  14.2 us (4%)
  other arithmetic  7.88 us (2%)
    unnamed x2, waiting for transfers between devices  75 us
    all_to_all x1, waiting for transfers between devices, body(): lax.all_to_all(outgoing.reshape(expert_count, capacity, -1), 'exp', split...  74.2 us
    pallas_call x1, Pallas kernels, attention(): pl.pallas_call(functools.partial(attention_kernel, sizes), out_shape=(jax...  70 us
    unnamed x19, local copies, waits for them, and re-layouts  20.1 us
    dot_general x1, matrix products, body(): lax.dot_general(scaled, weight, (((1,), (1,)), ((), ())), preferred_eleme...  11.1 us
    dot_general x1, matrix products, body(): outputs = jnp.dot(expert_rows, weight, preferred_element_type=jnp.float32)  8.61 us
    dot_general x1, matrix products, body(): lax.dot_general(expert_rows, scaled, (((0,), (0,)), ((), ())), preferred_...  6.53 us
  transfers between devices with their start and end apart: 4, of which 2 were waited for; matrix products, arithmetic and copies ran while one was open for 12% of the time, Pallas kernels for 22%

profile of v1, /device:TPU:0, one launch (start us, length us, event | category | flops | bytes accessed | tf_op | source)
XLA Modules:
  0.0 318.0 jit_solution(15832433026146759498)
XLA Ops:
  7.2 0.0 copy-start
  7.2 0.0 copy-start.3
  7.2 0.0 copy-start.6
  7.2 0.9 copy.52
  8.1 0.1 eq.65
  8.3 0.1 eq.61
  8.4 0.7 convert_element_type.75
  9.1 0.6 reduce-window.6
  9.7 0.2 slice_reduce_fusion
  9.9 0.1 fusion.28
  10.0 0.1 reduce_sum.50
  10.2 0.1 copy.54
  10.2 0.7 multiply_add_fusion
  10.9 0.3 fusion.19
  11.2 0.7 all_to_all.20
  11.9 5.9 %all-to-all-start = ((bf16[8,1,64]{2,1,0:T(2,128)(2,1)}), bf16[8,1,64]{2,1,0:T(2,128)(2,1)S(1)}, u32[]{:S(2)}, u32[]{:S(2)}) async-start(bf16[8,1,64]{2,1,0:T(2,128)(2,1)} %all_to_all.20), calls=%async_computation | async-start | bytes 8192 | tf_op jit(solution)/shard_map/all_to_all | solution.py:371
  17.8 0.1 convert_reduce_fusion
  17.9 0.9 reshape.136
  18.8 1.0 reshape.135
  19.8 2.4 copy.51.key_ref
  22.2 0.8 concatenate.3.rows_ref
  23.0 70.0 %shard_map.146 = (bf16[128,640]{1,0:T(8,128)(2,1)}, bf16[64,640]{1,0:T(8,128)(2,1)}) custom-call(bf16[64,1152]{1,0:T(8,128)(2,1)} %concatenate.3.rows_ref, bf16[1024,576]{1,0:T(8,128)(2,1)} %copy.51.key_ref), custom_call_target="tpu_custom_call" | custom-call | tf_op jit(solution)/shard_map/pallas_call | solution.py:280
  93.0 0.0 copy-done.3
  93.0 0.0 copy-done.6
  93.0 0.0 copy-start.4
  93.0 4.3 %fusion.5 = (f32[128]{0:T(128)S(1)}, f32[128]{0:T(128)S(1)}, f32[128,5120]{1,0:T(8,128)S(1)}) fusion(bf16[128,5120]{1,0:T(8,128)(2,1)S(1)} %copy-done.3, bf16[5120,576]{0,1:T(8,128)(2,1)} %param.16, bf16[128,640]{1,0:T(8,128)(2,1)} %get-tuple-element.8, f32[5120]{0:T(1024)S(1)} %copy-done.6), kind=kOutput, calls=%fused_computation.13 | convolution fusion | flops 758906624 | bytes 10015744 | tf_op jit(solution)/shard_map/dot_general | solution.py:330
  97.4 0.0 copy-done.4
  97.4 0.8 fusion.9
  98.2 0.0 copy-start.2
  98.2 3.9 %convolution_convert_fusion.1 = bf16[512,5120]{1,0:T(8,128)(2,1)} fusion(bf16[128,5120]{1,0:T(8,128)(2,1)S(1)} %fusion.9, bf16[128,512]{1,0:T(8,128)(2,1)S(1)} %convert_reduce_fusion), kind=kOutput, calls=%fused_computation.7 | convolution fusion | flops 673710080 | bytes 6684672 | tf_op jit(solution)/shard_map/dot_general | solution.py:356
  102.1 0.0 all-to-all-done
  102.1 0.0 copy-done.2
  102.1 5.2 %all-to-all-start.1 = ((bf16[8,64,5120]{2,1,0:T(8,128)(2,1)}), bf16[8,64,5120]{2,1,0:T(8,128)(2,1)}, u32[]{:S(2)}, u32[]{:S(2)}) async-start(bf16[8,64,5120]{2,1,0:T(8,128)(2,1)} %bitcast.50), calls=%async_computation.1 | async-start | bytes 10485760 | tf_op jit(solution)/shard_map/all_to_all | solution.py:364
  107.3 0.2 reduce-scatter.4.cloned.1.call-start
  107.5 74.2 %all-to-all-done.1 = bf16[8,64,5120]{2,1,0:T(8,128)(2,1)} async-done(((bf16[8,64,5120]{2,1,0:T(8,128)(2,1)}), bf16[8,64,5120]{2,1,0:T(8,128)(2,1)}, u32[]{:S(2)}, u32[]{:S(2)}) %all-to-all-start.1) | async-done | bytes 5242912 | tf_op jit(solution)/shard_map/all_to_all | solution.py:364
  181.7 4.1 %multiply_convert_fusion = bf16[8,64,5120]{2,1,0:T(8,128)(2,1)S(1)} fusion(f32[8,64]{1,0:T(8,128)S(1)} %bitcast.55, bf16[8,64,5120]{2,1,0:T(8,128)(2,1)} %all-to-all-done.1), kind=kLoop, calls=%fused_computation.2 | loop fusion | flops 7864320 | bytes 10487808 | tf_op jit(solution)/shard_map/convert_element_type | solution.py:383
  185.8 0.0 copy-start.1
  185.9 2.3 copy-done.1
  188.2 0.0 copy-done
  188.2 6.5 %fusion.4 = bf16[768,5120]{0,1:T(8,128)(2,1)} fusion(bf16[512,5120]{1,0:T(8,128)(2,1)S(1)} %bitcast.52, bf16[1,512,768]{2,1,0:T(8,128)(2,1)S(1)} %copy-done), kind=kOutput, calls=%fused_computation.8 | convolution fusion | flops 4030464000 | bytes 13893632 | tf_op jit(solution)/shard_map/dot_general | solution.py:396
  194.7 10.6 %copy.59 = bf16[768,5120]{1,0:T(8,128)(2,1)} copy(bf16[768,5120]{0,1:T(8,128)(2,1)} %fusion.4) | data formatting | bytes 15728640
  205.3 0.0 copy-start.5
  205.3 0.0 reduce-scatter.4.cloned.1.call-update
  205.4 0.9 copy-done.5
  206.2 0.7 reshape.137
  207.0 8.6 %fusion = f32[512]{0:T(512)S(1)} fusion(bf16[1,768,5120]{2,1,0:T(8,128)(2,1)} %param.21, bf16[8,64,5120]{2,1,0:T(8,128)(2,1)} %all-to-all-done.1, bf16[1,512,768]{2,1,0:T(8,128)(2,1)S(1)} %copy-done), kind=kOutput, calls=%fused_computation.1 | convolution fusion | flops 4034395648 | bytes 13895680 | tf_op jit(solution)/shard_map/dot_general | solution.py:389
  215.6 0.7 all_to_all.18
  216.3 3.9 %all-to-all-start.2 = ((f32[8,1,64]{2,1,0:T(1,128)}), f32[8,1,64]{2,1,0:T(1,128)S(1)}, u32[]{:S(2)}, u32[]{:S(2)}) async-start(f32[8,1,64]{2,1,0:T(1,128)} %all_to_all.18), calls=%async_computation.2 | async-start | bytes 8192 | tf_op jit(solution)/shard_map/all_to_all | solution.py:391
  220.1 11.1 %fusion.14 = bf16[1,512,768]{2,1,0:T(8,128)(2,1)} fusion(bf16[512,5120]{1,0:T(8,128)(2,1)} %bitcast.53, bf16[1,768,5120]{2,1,0:T(8,128)(2,1)} %param.21), kind=kOutput, calls=%fused_computation.20 | convolution fusion | flops 4026925056 | bytes 13893632 | tf_op jit(solution)/shard_map/dot_general | solution.py:386
  231.2 0.0 all-to-all-done.2
  231.2 0.5 broadcast.86
  231.7 0.7 reduce.5
  232.4 0.1 reshape.145
  232.5 0.8 fusion.21
  233.3 74.9 %reduce-scatter.4.cloned.1.call-done = bf16[48,5120]{1,0:T(8,128)(2,1)} async-done(((bf16[768,5120]{1,0:T(8,128)(2,1)}), bf16[48,5120]{1,0:T(8,128)(2,1)}) %reduce-scatter.4.cloned.1.call-update) | async-done | bytes 491536
  308.3 1.6 copy.60
  309.9 1.3 copy.56
  (7 shorter events, 0.1 us)
Async XLA Ops:
  7.2 181.0 %copy-start = (bf16[1,512,768]{2,1,0:T(8,128)(2,1)S(1)}, bf16[1,512,768]{2,1,0:T(8,128)(2,1)}, u32[]{:S(2)}) copy-start(bf16[1,512,768]{2,1,0:T(8,128)(2,1)} %param.20) | copy-start | bytes 2359300
  7.2 85.8 %copy-start.3 = (bf16[128,5120]{1,0:T(8,128)(2,1)S(1)}, bf16[128,5120]{1,0:T(8,128)(2,1)}, u32[]{:S(2)}) copy-start(bf16[128,5120]{1,0:T(8,128)(2,1)} %param.14) | copy-start | bytes 3932164
  7.2 85.8 %copy-start.6 = (f32[5120]{0:T(1024)S(1)}, f32[5120]{0:T(1024)}, u32[]{:S(2)}) copy-start(f32[5120]{0:T(1024)} %param.15) | copy-start | bytes 61444
  11.9 90.2 %all-to-all-start = ((bf16[8,1,64]{2,1,0:T(2,128)(2,1)}), bf16[8,1,64]{2,1,0:T(2,128)(2,1)S(1)}, u32[]{:S(2)}, u32[]{:S(2)}) async-start(bf16[8,1,64]{2,1,0:T(2,128)(2,1)} %all_to_all.20), calls=%async_computation | async-start | bytes 8192 | tf_op jit(solution)/shard_map/all_to_all | solution.py:371
  93.0 4.4 %copy-start.4 = (bf16[128,5120]{1,0:T(8,128)(2,1)S(1)}, bf16[128,5120]{1,0:T(8,128)(2,1)}, u32[]{:S(2)}) copy-start(bf16[128,5120]{1,0:T(8,128)(2,1)} %param.17) | copy-start | bytes 3932164
  98.2 3.9 %copy-start.2 = (bf16[128,5120]{1,0:T(8,128)(2,1)}, bf16[128,5120]{1,0:T(8,128)(2,1)S(1)}, u32[]{:S(2)}) copy-start(bf16[128,5120]{1,0:T(8,128)(2,1)S(1)} %fusion.9) | copy-start | bytes 3932164
  102.1 79.6 %all-to-all-start.1 = ((bf16[8,64,5120]{2,1,0:T(8,128)(2,1)}), bf16[8,64,5120]{2,1,0:T(8,128)(2,1)}, u32[]{:S(2)}, u32[]{:S(2)}) async-start(bf16[8,64,5120]{2,1,0:T(8,128)(2,1)} %bitcast.50), calls=%async_computation.1 | async-start | bytes 10485760 | tf_op jit(solution)/shard_map/all_to_all | solution.py:364
  107.3 200.9 %reduce-scatter.4.cloned.1.call-start = ((), (), s32[]{:S(2)}) async-start(), calls=%async_computation.4 | async-start | bytes 8355840
  185.8 2.3 copy-start.1
  205.3 0.9 copy-start.5
  216.3 14.9 %all-to-all-start.2 = ((f32[8,1,64]{2,1,0:T(1,128)}), f32[8,1,64]{2,1,0:T(1,128)S(1)}, u32[]{:S(2)}, u32[]{:S(2)}) async-start(f32[8,1,64]{2,1,0:T(1,128)} %all_to_all.18), calls=%async_computation.2 | async-start | bytes 8192 | tf_op jit(solution)/shard_map/all_to_all | solution.py:391
Sparse Core Ops, SparseCore 0:
  205.5 102.7 reduce-scatter.3

commit v2 on v1

--- a/solution.py
+++ b/solution.py
@@ -313,6 +313,282 @@
     return query_grad, key_rows[:, :key_width]
 
 
+def expert_kernel(
+    sizes,
+    stream_ref,
+    placing_ref,
+    slot_weights_ref,
+    acts_ref,
+    proj_hbm,
+    act_out,
+    down_out,
+    returned,
+    proj,
+    outgoing,
+    arrived,
+    weights_in,
+    acts_t,
+    through,
+    partial,
+    core_in,
+    x_in,
+    z_part,
+    z_in,
+    slot_parts,
+    proj_sem,
+    slot_send,
+    slot_recv,
+    weight_send,
+    weight_recv,
+    core_send,
+    core_recv,
+    x_send,
+    x_recv,
+    z_send,
+    z_recv,
+    back_send,
+    back_recv,
+):
+    n_ctx, n_exp, chunks, n_x, n_z = sizes
+    me = lax.axis_index("ctx")
+    mine = lax.axis_index("exp")
+    core = lax.rem(me, 2)
+    z_at = lax.rem(me // 2, n_z)
+    x_at = me // (2 * n_z)
+    depth = stream_ref.shape[1] // chunks
+    slots, inner = acts_ref.shape
+    capacity = slots // n_exp
+    chips = n_ctx // 2
+    share = inner // n_ctx
+
+    def columns(c):
+        return pl.ds(pl.multiple_of(c * depth, depth), depth)
+
+    def proj_copy(c):
+        return pltpu.make_async_copy(proj_hbm.at[:, columns(c)], proj.at[c], proj_sem.at[c])
+
+    @pl.loop(0, chunks)
+    def _(c):
+        proj_copy(c).start()
+
+    greet((("ctx", n_ctx), ("exp", n_exp)))
+
+    def weight_copy(there, source):
+        return push(
+            slot_weights_ref.at[there],
+            weights_in.at[source],
+            weight_send.at[there],
+            weight_recv.at[source],
+            {"exp": there},
+        )
+
+    def slot_copy(c, there, source):
+        return push(
+            outgoing.at[c, there],
+            arrived.at[c, source],
+            slot_send.at[c, there],
+            slot_recv.at[c, source],
+            {"exp": there},
+        )
+
+    def core_copy(c):
+        return push(
+            partial.at[c, 1 - core], core_in.at[c], core_send.at[c], core_recv.at[c], {"ctx": me + 1 - 2 * core}
+        )
+
+    def x_copy(c, there, source):
+        return push(
+            partial.at[c, core, there],
+            x_in.at[c, source],
+            x_send.at[c, there],
+            x_recv.at[c, source],
+            {"ctx": (there * n_z + z_at) * 2 + core},
+        )
+
+    def z_copy(c):
+        return push(
+            z_part.at[c, 1 - z_at],
+            z_in.at[c],
+            z_send.at[c],
+            z_recv.at[c],
+            {"ctx": (x_at * n_z + 1 - z_at) * 2 + core},
+        )
+
+    def back_copy(there, source):
+        return push(
+            slot_parts.at[there], returned.at[source], back_send.at[there], back_recv.at[source], {"exp": there}
+        )
+
+    @pl.loop(1, n_exp)
+    def _(k):
+        weight_copy(lax.rem(mine + k, n_exp), mine).start()
+
+    weights_in[mine] = slot_weights_ref[mine]
+
+    @pl.loop(0, chunks)
+    def _(c):
+        placed = jnp.dot(placing_ref[...], stream_ref[:, columns(c)], preferred_element_type=F32)
+        outgoing[c] = placed.astype(BF16).reshape(n_exp, capacity, depth)
+
+        @pl.loop(1, n_exp)
+        def _(k):
+            slot_copy(c, lax.rem(mine + k, n_exp), mine).start()
+
+        arrived[c, mine] = outgoing[c, mine]
+
+    @pl.loop(1, n_exp)
+    def _(k):
+        weight_copy(mine, lax.rem(mine + k, n_exp)).wait_recv()
+
+    slot_weight = weights_in[...].reshape(slots, LANES).astype(F32)[:, :1]
+    turned = (acts_ref[...].astype(F32) * slot_weight).T.astype(BF16)
+    for q in range(chips):
+        for s in range(2):
+            at = (q * 2 + s) * share
+            to = (s * chips + q) * share
+            acts_t[to : to + share] = turned[at : at + share]
+
+    through[...] = jnp.zeros(through.shape, F32)
+
+    @pl.loop(0, chunks + 3)
+    def _(c):
+        @pl.when(c < chunks)
+        def _():
+            @pl.loop(1, n_exp)
+            def _(k):
+                slot_copy(c, mine, lax.rem(mine + k, n_exp)).wait_recv()
+
+            proj_copy(c).wait()
+            rows = arrived[c].reshape(slots, depth)
+            down = jnp.dot(acts_t[...], rows, preferred_element_type=F32)
+            partial[c] = down.astype(BF16).reshape(2, n_x, n_z, share, depth)
+            core_copy(c).start()
+            through[...] += nt_dot(rows, proj[c])
+
+        @pl.when((c >= 1) & (c < chunks + 1))
+        def _():
+            d = c - 1
+            core_copy(d).wait_recv()
+            total = partial[d, core].astype(F32) + core_in[d].astype(F32)
+            partial[d, core] = total.astype(BF16)
+            x_in[d, x_at] = partial[d, core, x_at]
+
+            @pl.loop(1, n_x)
+            def _(k):
+                x_copy(d, lax.rem(x_at + k, n_x), x_at).start()
+
+        @pl.when((c >= 2) & (c < chunks + 2))
+        def _():
+            d = c - 2
+
+            @pl.loop(1, n_x)
+            def _(k):
+                x_copy(d, x_at, lax.rem(x_at + k, n_x)).wait_recv()
+
+            total = x_in[d, 0].astype(F32)
+            for k in range(1, n_x):
+                total = total + x_in[d, k].astype(F32)
+            z_part[d] = total.astype(BF16)
+            z_copy(d).start()
+
+        @pl.when(c >= 3)
+        def _():
+            d = c - 3
+            z_copy(d).wait_recv()
+            total = z_part[d, z_at].astype(F32) + z_in[d].astype(F32)
+            down_out[:, columns(d)] = total.astype(BF16)
+
+        @pl.when(c == chunks - 1)
+        def _():
+            all_through = through[...]
+            act_out[...] = (all_through * slot_weight).astype(BF16)
+            sums = jnp.sum(acts_ref[...].astype(F32) * all_through, axis=1, keepdims=True)
+            slot_parts[...] = jnp.broadcast_to(sums, (slots, LANES)).reshape(slot_parts.shape)
+
+            @pl.loop(1, n_exp)
+            def _(k):
+                back_copy(lax.rem(mine + k, n_exp), mine).start()
+
+            returned[mine] = slot_parts[mine]
+
+    @pl.loop(1, n_exp)
+    def _(k):
+        there = lax.rem(mine + k, n_exp)
+        back_copy(mine, there).wait_recv()
+        back_copy(there, mine).wait_send()
+        weight_copy(there, mine).wait_send()
+
+    @pl.loop(0, chunks)
+    def _(c):
+        @pl.loop(1, n_exp)
+        def _(k):
+            slot_copy(c, lax.rem(mine + k, n_exp), mine).wait_send()
+
+        core_copy(c).wait_send()
+
+        @pl.loop(1, n_x)
+        def _(k):
+            x_copy(c, lax.rem(x_at + k, n_x), x_at).wait_send()
+
+        z_copy(c).wait_send()
+
+
+def experts(stream_total, placing, slot_weights, acts, proj):
+    n_ctx, n_exp = lax.axis_size("ctx"), lax.axis_size("exp")
+    slots, inner = acts.shape
+    width = stream_total.shape[1]
+    capacity = slots // n_exp
+    chunks = 10
+    n_z = 2
+    n_x = n_ctx // (2 * n_z)
+    depth = width // chunks
+    share = inner // n_ctx
+    chips = n_ctx // 2
+    wide_weights = jnp.broadcast_to(slot_weights[:, None], (slots, LANES)).reshape(n_exp, capacity, LANES)
+    vmem = pl.BlockSpec(memory_space=pltpu.VMEM)
+    dma = pltpu.SemaphoreType.DMA
+    return pl.pallas_call(
+        functools.partial(expert_kernel, (n_ctx, n_exp, chunks, n_x, n_z)),
+        out_shape=(
+            jax.ShapeDtypeStruct((slots, inner), BF16),
+            jax.ShapeDtypeStruct((share, width), BF16),
+            jax.ShapeDtypeStruct((n_exp, capacity, LANES), F32),
+        ),
+        in_specs=[vmem, vmem, vmem, vmem, pl.BlockSpec(memory_space=pl.ANY)],
+        out_specs=(vmem, vmem, vmem),
+        scratch_shapes=[
+            pltpu.VMEM((chunks, inner, depth), BF16),
+            pltpu.VMEM((chunks, n_exp, capacity, depth), BF16),
+            pltpu.VMEM((chunks, n_exp, capacity, depth), BF16),
+            pltpu.VMEM((n_exp, capacity, LANES), BF16),
+            pltpu.VMEM((inner, slots), BF16),
+            pltpu.VMEM((slots, inner), F32),
+            pltpu.VMEM((chunks, 2, n_x, n_z, share, depth), BF16),
+            pltpu.VMEM((chunks, n_x, n_z, share, depth), BF16),
+            pltpu.VMEM((chunks, n_x, n_z, share, depth), BF16),
+            pltpu.VMEM((chunks, n_z, share, depth), BF16),
+            pltpu.VMEM((chunks, share, depth), BF16),
+            pltpu.VMEM((n_exp, capacity, LANES), F32),
+            dma((chunks,)),
+            dma((chunks, n_exp)),
+            dma((chunks, n_exp)),
+            dma((n_exp,)),
+            dma((n_exp,)),
+            dma((chunks,)),
+            dma((chunks,)),
+            dma((chunks, n_x)),
+            dma((chunks, n_x)),
+            dma((chunks,)),
+            dma((chunks,)),
+            dma((n_exp,)),
+            dma((n_exp,)),
+        ],
+        compiler_params=pltpu.CompilerParams(
+            collective_id=1, has_side_effects=True, vmem_limit_bytes=60 * 2**20
+        ),
+    )(stream_total, placing, wide_weights, acts, proj)
+
+
 def body(
     queries,
     latents,
@@ -353,53 +629,14 @@
     )
     select = select.reshape(local_rows, top_count, slot_count)
     placing = jnp.sum(select, axis=1).astype(jnp.bfloat16)
-    outgoing = lax.dot_general(
-        placing, stream_total, (((0,), (0,)), ((), ())), preferred_element_type=jnp.float32
-    ).astype(jnp.bfloat16)
     rounded_weights = lax.optimization_barrier(route_weights.astype(jnp.bfloat16)).astype(
         jnp.float32
     )
     weight_slots = jnp.einsum("tks,tk->s", select, rounded_weights).astype(jnp.bfloat16)
-    arrived, arrived_weights = (
-        lax.all_to_all(
-            outgoing.reshape(expert_count, capacity, -1),
-            "exp",
-            split_axis=0,
-            concat_axis=0,
-            tiled=True,
-        ),
-        lax.all_to_all(
-            weight_slots.reshape(expert_count, capacity),
-            "exp",
-            split_axis=0,
-            concat_axis=0,
-            tiled=True,
-        ),
-    )
-    arrived = arrived.reshape(slot_count, -1)
-    arrived_weights = arrived_weights.reshape(slot_count)
-    expert_rows = expert_acts[0]
-    weight = down_proj[0]
-    scaled = (arrived_weights.astype(jnp.float32)[:, None] * arrived.astype(jnp.float32)).astype(
-        jnp.bfloat16
-    )
-    act_grad = lax.dot_general(
-        scaled, weight, (((1,), (1,)), ((), ())), preferred_element_type=jnp.float32
-    ).astype(jnp.bfloat16)
-    outputs = jnp.dot(expert_rows, weight, preferred_element_type=jnp.float32)
-    slot_grads = jnp.sum(arrived.astype(jnp.float32) * outputs, axis=1)
-    returned = lax.all_to_all(
-        slot_grads.reshape(expert_count, capacity), "exp", split_axis=0, concat_axis=0, tiled=True
-    ).reshape(slot_count)
-    weight_grad = jnp.einsum("tks,s->tk", select, returned)
-    down_share = lax.psum_scatter(
-        lax.dot_general(
-            expert_rows, scaled, (((0,), (0,)), ((), ())), preferred_element_type=jnp.float32
-        ).astype(jnp.bfloat16),
-        "ctx",
-        scatter_dimension=0,
-        tiled=True,
-    )
+    act_grad, down_share, returned = experts(
+        stream_total, placing.T, weight_slots, expert_acts[0], down_proj[0]
+    )
+    weight_grad = jnp.einsum("tks,s->tk", select, returned[:, :, 0].reshape(slot_count))
     return (query_grad, stream_total, act_grad[None], down_share[None], weight_grad)
 
 

time: 319 us -> 212 us (0.66)
  waiting for transfers between devices: 149 us -> 0 us
  Pallas kernels: 70 us -> 186 us
  matrix products: 35.5 us -> 5.43 us
  starting transfers between devices: 15.2 us -> 0 us
  between operations: 14.2 us -> 0.75 us
  local copies, waits for them, and re-layouts: 26.1 us -> 14.3 us
  other arithmetic: 7.88 us -> 2.79 us
    pallas_call x0 -> x1, Pallas kernels: none -> 116 us  [experts(): pl.pallas_call(functools.partial(expert_kernel, (n_ctx, n_exp, chunks, n_...]
    unnamed x2 -> x0, waiting for transfers between devices: 75 us -> none
    all_to_all x3 -> x0, waiting for transfers between devices: 74.2 us -> none  [the longest x1 74.2 us: body(): lax.all_to_all(outgoing.reshape(expert_count, capacity, -1), 'exp', split...]
    dot_general x5 -> x1, matrix products: 30.9 us -> 0.83 us  [body(): jnp.einsum('tks,s->tk', select, returned[:, :, 0].reshape(slot_count))]
    all_to_all x3 -> x0, starting transfers between devices: 15 us -> none  [the longest x1 5.91 us: body(): lax.all_to_all(weight_slots.reshape(expert_count, capacity), 'exp', split...]
    unnamed x19 -> x14, local copies, waits for them, and re-layouts: 20.1 us -> 6.43 us
    convert_element_type x2 -> x0, other arithmetic: 4.15 us -> none  [the longest x1 4.14 us: body(): (arrived_weights.astype(jnp.float32)[:, None] * arrived.astype(jnp.float3...]
  transfers between devices with their start and end apart: 4 -> 0, of which waited for: 2 -> 0; matrix products, arithmetic and copies ran while one was open for 12% -> 0% of each run, Pallas kernels for 22% -> 0%
where the time goes in v2:
time: 212 us; the launch traced here: 209 us
  Pallas kernels  186 us (88%)
  local copies, waits for them, and re-layouts  14.3 us (7%)
  matrix products  5.43 us (3%)
  other arithmetic  2.79 us (1%)
    pallas_call x1, Pallas kernels, experts(): pl.pallas_call(functools.partial(expert_kernel, (n_ctx, n_exp, chunks, n_...  116 us
    pallas_call x1, Pallas kernels, attention(): pl.pallas_call(functools.partial(attention_kernel, sizes), out_shape=(jax...  70.5 us
    unnamed x14, local copies, waits for them, and re-layouts  6.43 us
    dot_general x1, matrix products, body(): lax.dot_general(key_rows, latent_proj, (((1,), (1,)), ((), ())), preferre...  4.34 us

profile of v2, /device:TPU:0, one launch (start us, length us, event | category | flops | bytes accessed | tf_op | source)
XLA Modules:
  0.0 209.4 jit_solution(1344422261627412552)
XLA Ops:
  0.6 0.0 copy-start
  0.6 0.0 copy-start.2
  0.7 1.1 reshape.103
  1.8 0.9 reshape.104
  2.7 0.8 concatenate.3.rows_ref
  3.4 2.4 %copy.33.key_ref = bf16[1024,576]{1,0:T(8,128)(2,1)} copy(bf16[1024,576]{0,1:T(8,128)(2,1)} %param.12) | data formatting | bytes 2359296 | tf_op args[1]
  5.8 70.5 %shard_map.146 = (bf16[128,640]{1,0:T(8,128)(2,1)}, bf16[64,640]{1,0:T(8,128)(2,1)}) custom-call(bf16[64,1152]{1,0:T(8,128)(2,1)} %concatenate.3.rows_ref, bf16[1024,576]{1,0:T(8,128)(2,1)} %copy.33.key_ref), custom_call_target="tpu_custom_call" | custom-call | tf_op jit(solution)/shard_map/pallas_call | solution.py:280
  76.3 1.6 reshape.105
  77.9 0.0 copy-done
  77.9 0.0 copy-done.2
  78.0 0.0 copy-start.1
  78.0 4.3 %fusion = (f32[128]{0:T(128)S(1)}, f32[128]{0:T(128)S(1)}, f32[128,5120]{1,0:T(8,128)S(1)}) fusion(bf16[128,5120]{1,0:T(8,128)(2,1)S(1)} %copy-done, bf16[5120,576]{0,1:T(8,128)(2,1)} %param.16, bf16[128,640]{1,0:T(8,128)(2,1)} %get-tuple-element.11, f32[5120]{0:T(1024)S(1)} %copy-done.2), kind=kOutput, calls=%fused_computation.4 | convolution fusion | flops 758906624 | bytes 10015744 | tf_op jit(solution)/shard_map/dot_general | solution.py:606
  82.3 0.0 copy-done.1
  82.3 0.0 copy-start.3
  82.3 0.0 copy-start.4
  82.3 1.9 fusion.4.stream_ref
  84.2 0.0 copy-done.3
  84.2 0.1 copy.34
  84.4 0.1 eq.65
  84.5 0.6 reduce-window.6
  85.1 0.2 slice_reduce_fusion.1
  85.4 0.1 eq.61
  85.5 0.1 fusion.14
  85.6 0.1 reduce_sum.41
  85.7 0.1 copy.36
  85.8 0.1 convert_reduce_fusion
  86.0 0.8 copy.37
  86.7 0.0 copy-done.4
  86.7 0.3 fusion.6
  87.0 0.1 broadcast_in_dim.11
  87.1 0.8 broadcast_in_dim.12.slot_weights_ref
  87.9 115.6 %shard_map.147 = (bf16[512,768]{1,0:T(8,128)(2,1)}, bf16[48,5120]{1,0:T(8,128)(2,1)}, f32[8,64,128]{2,1,0:T(8,128)}) custom-call(bf16[128,5120]{1,0:T(8,128)(2,1)} %fusion.4.stream_ref, bf16[512,128]{1,0:T(8,128)(2,1)} %bitcast.29, bf16[8,64,128]{2,1,0:T(8,128)(2,1)} %broadcast_in_dim.12.slot_weights_ref, bf16[512,768]{1,0:T(8,128)(2,1)} %bitcast.27, ...), custom_call_target="tpu_custom_call" | custom-call | tf_op jit(solution)/shard_map/pallas_call | solution.py:550
  203.5 1.1 slice_reduce_fusion
  204.6 0.1 reshape.109
  204.7 0.8 fusion.8
  205.5 2.1 copy.44
  207.6 1.8 copy.45
  (8 shorter events, 0.1 us)
Async XLA Ops:
  0.6 77.3 %copy-start = (bf16[128,5120]{1,0:T(8,128)(2,1)S(1)}, bf16[128,5120]{1,0:T(8,128)(2,1)}, u32[]{:S(2)}) copy-start(bf16[128,5120]{1,0:T(8,128)(2,1)} %param.14) | copy-start | bytes 3932164
  0.6 77.3 %copy-start.2 = (f32[5120]{0:T(1024)S(1)}, f32[5120]{0:T(1024)}, u32[]{:S(2)}) copy-start(f32[5120]{0:T(1024)} %param.15) | copy-start | bytes 61444
  78.0 4.4 %copy-start.1 = (bf16[128,5120]{1,0:T(8,128)(2,1)S(1)}, bf16[128,5120]{1,0:T(8,128)(2,1)}, u32[]{:S(2)}) copy-start(bf16[128,5120]{1,0:T(8,128)(2,1)} %param.17) | copy-start | bytes 3932164
  82.3 1.9 copy-start.3
  82.3 4.4 %copy-start.4 = (f32[128,2]{0,1:T(2,128)S(1)}, f32[128,2]{0,1:T(2,128)}, u32[]{:S(2)}) copy-start(f32[128,2]{0,1:T(2,128)} %param.19) | copy-start | bytes 3076

commit v3 on v2

--- a/solution.py
+++ b/solution.py
@@ -48,11 +48,23 @@
     pl.semaphore_wait(barrier, total)
 
 
+def meet(peers):
+    barrier = pltpu.get_barrier_semaphore()
+    for where in peers:
+        pl.semaphore_signal(barrier, inc=1, device_id=where, device_id_type=MESH)
+    pl.semaphore_wait(barrier, len(peers))
+
+
 def attention_kernel(
     sizes,
-    rows_ref,
-    key_ref,
-    key_out,
+    queries_ref,
+    out_grad_ref,
+    latents_t_ref,
+    gain_ref,
+    hidden_hbm,
+    stream_hbm,
+    proj_t_hbm,
+    stream_out,
     query_out,
     rows_all,
     stats_all,
@@ -62,56 +74,102 @@
     score_grads,
     key_parts,
     key_all,
-    query_parts,
-    query_all,
+    hidden,
+    stream,
+    proj_t,
+    load_sem,
     rows_send,
     rows_recv,
+    pass_send,
     stats_send,
     stats_recv,
     key_send,
     key_recv,
-    query_send,
-    query_recv,
 ):
     n_ctx, n_exp, key_width, value_width, query_rows, heads = sizes
     wide = padded(key_width)
     me = lax.axis_index("ctx")
     mine = lax.axis_index("exp")
-    key_count = key_ref.shape[0]
+    core = lax.rem(me, 2)
+    sibling = me + 1 - 2 * core
+    key_count = latents_t_ref.shape[1]
+    width = gain_ref.shape[1]
     per = query_rows * heads
     scale = key_width ** (-0.5)
     group = 4
     cols = group * per
     n_groups = n_ctx // group
     tiles = cols // LANES
+    first = me // group
+
+    hidden_load = pltpu.make_async_copy(hidden_hbm, hidden, load_sem.at[0])
+    proj_load = pltpu.make_async_copy(proj_t_hbm, proj_t.at[:key_width], load_sem.at[1])
+    stream_load = pltpu.make_async_copy(stream_hbm, stream, load_sem.at[2])
+    for copy in (hidden_load, proj_load, stream_load):
+        copy.start()
+
+    query_values = queries_ref[...].astype(F32)
+    grad_values = out_grad_ref[...].astype(F32)
+    rows_all[me, :, :key_width] = jnp.concatenate(
+        [query_values[:, h * key_width : (h + 1) * key_width] for h in range(heads)], axis=0
+    ).astype(BF16)
+    rows_all[me, :, key_width:wide] = jnp.zeros((per, wide - key_width), BF16)
+    rows_all[me, :, wide:] = jnp.concatenate(
+        [grad_values[:, h * value_width : (h + 1) * value_width] for h in range(heads)], axis=0
+    ).astype(BF16)
 
     greet((("ctx", n_ctx), ("exp", n_exp)))
 
     def rows_copy(there, source):
         return push(
-            rows_ref, rows_all.at[source], rows_send.at[there], rows_recv.at[source], {"ctx": there}
-        )
-
-    @pl.loop(0, me)
+            rows_all.at[source],
+            rows_all.at[source],
+            rows_send.at[there],
+            rows_recv.at[source],
+            {"ctx": there},
+        )
+
+    def pass_copy(source):
+        return push(
+            rows_all.at[source],
+            rows_all.at[source],
+            pass_send.at[source],
+            rows_recv.at[source],
+            {"ctx": sibling},
+        )
+
+    @pl.loop(0, me // 2)
     def _(i):
-        rows_copy(me - 1 - i, me).start()
+        rows_copy(me - 2 - 2 * i, me).start()
+
+    @pl.when(core == 1)
+    def _():
+        pass_copy(me).start()
 
     @pl.loop(0, me)
     def _(i):
         rows_all[i] = jnp.zeros(rows_all.shape[1:], BF16)
 
-    rows_all[me] = rows_ref[...]
-    keys[:, :key_width] = key_ref[...]
+    keys[:, :key_width] = latents_t_ref[...].T
     keys[:, key_width:] = jnp.zeros((key_count, wide - key_width), BF16)
-
-    @pl.loop(0, n_groups)
+    proj_t[key_width:] = jnp.zeros((wide - key_width, width), BF16)
+    stats_all[me, 0] = jnp.full(stats_all.shape[2:], NEG_LARGE, F32)
+    stats_all[me, 1] = jnp.zeros(stats_all.shape[2:], F32)
+    stats_all[me, 2] = jnp.zeros(stats_all.shape[2:], F32)
+
+    @pl.loop(0, first)
     def _(g):
-        for k in range(group):
-            b = g * group + k
+        at = pl.ds(pl.multiple_of(g * cols, cols), cols)
+        weights[:, at] = jnp.zeros((key_count, cols), F32)
+        grads[:, at] = jnp.zeros((key_count, cols), F32)
+
+    def compute(g):
+        for k in range(n_groups // 2):
+            b = g * group + 2 * k + 1 - core
 
             @pl.when(b > me)
             def _():
-                rows_copy(0, b).wait_recv()
+                pass_copy(b).wait_recv()
 
         block = rows_all[pl.ds(g * group, group)].reshape(cols, rows_all.shape[2])
         at = pl.ds(pl.multiple_of(g * cols, cols), cols)
@@ -122,7 +180,7 @@
             (g * group + column // per - me) * key_count
             + key_count
             - query_rows
-            + (column % per) // heads
+            + column % query_rows
         )
         visible = lax.broadcasted_iota(jnp.int32, (key_count, cols), 0) <= last
         masked = jnp.where(visible, scores, NEG_LARGE)
@@ -137,6 +195,22 @@
             for n, value in enumerate((top, total, dotted)):
                 stats_all[me, n, pl.ds(g * tiles + k, 1)] = value[:, part]
 
+    @pl.loop(first, n_groups + 1)
+    def _(g):
+        @pl.when(g < n_groups)
+        def _():
+            for k in range(n_groups // 2):
+                b = g * group + 2 * k + core
+
+                @pl.when(b > me)
+                def _():
+                    rows_copy(0, b).wait_recv()
+                    pass_copy(b).start()
+
+        @pl.when(g > first)
+        def _():
+            compute(g - 1)
+
     def stats_copy(there, source):
         return push(
             stats_all.at[source],
@@ -146,11 +220,18 @@
             {"ctx": there},
         )
 
-    @pl.loop(0, n_ctx)
+    @pl.loop(1, n_ctx)
     def _(i):
-        @pl.when(i != me)
-        def _():
-            stats_copy(i, me).start()
+        stats_copy(lax.rem(me + i, n_ctx), me).start()
+
+    hidden_load.wait()
+    proj_load.wait()
+    hidden_values = hidden[...].astype(F32)
+    inverse = lax.rsqrt(jnp.mean(hidden_values * hidden_values, axis=1, keepdims=True) + EPSILON)
+    gained = hidden_values * gain_ref[...]
+    high = gained.astype(BF16)
+    low = (gained - high.astype(F32)).astype(BF16)
+    pulled = (nt_dot(high, proj_t[...]) + nt_dot(low, proj_t[...])) * (1.0 / width)
 
     @pl.loop(0, n_ctx)
     def _(i):
@@ -174,9 +255,11 @@
 
     piece = key_count // n_exp
     step = 2 * piece
-
-    @pl.loop(0, key_count // step)
-    def _(n):
+    steps = key_count // step
+
+    @pl.loop(1, steps + 1)
+    def _(turn):
+        n = lax.rem(mine // 2 + turn, steps)
         at = pl.ds(pl.multiple_of(n * step, step), step)
         probs = weights[at, :] * share_row
         now = (probs * (grads[at, :] - delta_row)).astype(BF16)
@@ -197,26 +280,13 @@
 
     key_all[mine] = key_parts[mine]
 
-    def query_copy(there, source):
-        return push(
-            query_parts.at[there],
-            query_all.at[source],
-            query_send.at[there],
-            query_recv.at[source],
-            {"ctx": there},
-        )
-
     @pl.loop(0, n_groups)
     def _(g):
         at = pl.ds(pl.multiple_of(g * cols, cols), cols)
         part = tn_dot(score_grads[:, at], keys[...]) * scale
-        query_parts[pl.ds(g * group, group)] = part.astype(BF16).reshape(group, per, wide)
+        parts = part.astype(BF16).reshape(group, per, wide)
         for k in range(group):
-            b = g * group + k
-
-            @pl.when(b > me)
-            def _():
-                query_copy(b, me).start()
+            query_out[k % 2, g * (group // 2) + k // 2] = parts[k]
 
     @pl.loop(0, n_exp)
     def _(s):
@@ -227,27 +297,38 @@
     key_total = key_all[0].astype(F32)
     for s in range(1, n_exp):
         key_total = key_total + key_all[s].astype(F32)
-    key_out[...] = key_total.astype(BF16)
-
-    def add(i, so_far):
-        query_copy(me, i).wait_recv()
-        return so_far + query_all[i].astype(F32)
-
-    query_out[...] = lax.fori_loop(0, me, add, query_parts[me].astype(F32)).astype(BF16)
-
-    @pl.loop(0, me)
+    key_rows = key_total.astype(BF16)
+    aligned = jnp.sum(key_rows.astype(F32) * pulled, axis=1, keepdims=True)
+    back = inverse * inverse * inverse * aligned
+    stream_load.wait()
+    depth = 512
+
+    @pl.loop(0, width // depth)
+    def _(c):
+        at = pl.ds(pl.multiple_of(c * depth, depth), depth)
+        norm_grad = jnp.dot(key_rows, proj_t[:, at], preferred_element_type=F32)
+        through_norm = inverse * (gain_ref[:, at] * norm_grad) - hidden[:, at].astype(F32) * back
+        stream_out[:, at] = (stream[:, at].astype(F32) + through_norm).astype(BF16)
+
+    @pl.loop(0, me // 2)
     def _(i):
-        rows_copy(i, me).wait_send()
-
-    @pl.loop(0, n_ctx)
+        rows_copy(me - 2 - 2 * i, me).wait_send()
+
+    @pl.when(core == 1)
+    def _():
+        pass_copy(me).wait_send()
+
+    @pl.loop(0, n_ctx // 2)
     def _(i):
-        @pl.when(i != me)
-        def _():
-            stats_copy(i, me).wait_send()
-
-        @pl.when(i > me)
-        def _():
-            query_copy(i, me).wait_send()
+        b = 2 * i + core
+
+        @pl.when(b > me)
+        def _():
+            pass_copy(b).wait_send()
+
+    @pl.loop(1, n_ctx)
+    def _(i):
+        stats_copy(lax.rem(me + i, n_ctx), me).wait_send()
 
     @pl.loop(0, n_exp)
     def _(s):
@@ -256,7 +337,7 @@
             key_copy(s, mine).wait_send()
 
 
-def attention(queries, latents, out_grad):
+def attention(queries, latents, out_grad, hidden_rows, norm_gain, latent_proj, stream_grad):
     key_count, key_width = latents.shape
     query_rows = queries.shape[0]
     heads = queries.shape[1] // key_width
@@ -266,24 +347,18 @@
     n_ctx, n_exp = lax.axis_size("ctx"), lax.axis_size("exp")
     piece = key_count // n_exp
     total_rows = n_ctx * per
-    rows = jnp.concatenate(
-        [
-            queries.reshape(per, key_width),
-            jnp.zeros((per, wide - key_width), BF16),
-            out_grad.reshape(per, value_width),
-        ],
-        axis=1,
-    )
+    token_rows, width = hidden_rows.shape
     sizes = (n_ctx, n_exp, key_width, value_width, query_rows, heads)
     vmem = pl.BlockSpec(memory_space=pltpu.VMEM)
+    hbm = pl.BlockSpec(memory_space=pl.ANY)
     dma = pltpu.SemaphoreType.DMA
-    key_rows, query_grad = pl.pallas_call(
+    return pl.pallas_call(
         functools.partial(attention_kernel, sizes),
         out_shape=(
-            jax.ShapeDtypeStruct((piece, wide), BF16),
-            jax.ShapeDtypeStruct((per, wide), BF16),
+            jax.ShapeDtypeStruct((token_rows, width), BF16),
+            jax.ShapeDtypeStruct((2, n_ctx // 2, per, wide), BF16),
         ),
-        in_specs=[vmem, vmem],
+        in_specs=[vmem, vmem, vmem, vmem, hbm, hbm, hbm],
         out_specs=(vmem, vmem),
         scratch_shapes=[
             pltpu.VMEM((n_ctx, per, wide + value_width), BF16),
@@ -294,36 +369,51 @@
             pltpu.VMEM((key_count, total_rows), BF16),
             pltpu.VMEM((n_exp, piece, wide), BF16),
             pltpu.VMEM((n_exp, piece, wide), BF16),
-            pltpu.VMEM((n_ctx, per, wide), BF16),
-            pltpu.VMEM((n_ctx, per, wide), BF16),
+            pltpu.VMEM((token_rows, width), BF16),
+            pltpu.VMEM((token_rows, width), BF16),
+            pltpu.VMEM((wide, width), BF16),
+            dma((3,)),
+            dma((n_ctx,)),
             dma((n_ctx,)),
             dma((n_ctx,)),
             dma((n_ctx,)),
             dma((n_ctx,)),
             dma((n_exp,)),
             dma((n_exp,)),
-            dma((n_ctx,)),
-            dma((n_ctx,)),
         ],
         compiler_params=pltpu.CompilerParams(
-            collective_id=0, has_side_effects=True, vmem_limit_bytes=56 * 2**20
+            collective_id=0, has_side_effects=True, vmem_limit_bytes=58 * 2**20
         ),
-    )(rows, latents)
-    query_grad = query_grad[:, :key_width].reshape(query_rows, heads * key_width)
-    return query_grad, key_rows[:, :key_width]
+    )(
+        queries,
+        out_grad,
+        latents.T,
+        norm_gain.reshape(1, width),
+        hidden_rows,
+        stream_grad,
+        latent_proj.T,
+    )
 
 
 def expert_kernel(
     sizes,
     stream_ref,
-    placing_ref,
-    slot_weights_ref,
+    query_ref,
+    ids_ref,
+    route_ref,
     acts_ref,
     proj_hbm,
     act_out,
     down_out,
+    weight_out,
+    query_out,
+    proj,
+    placing,
+    slot_weights,
     returned,
-    proj,
+    query_in,
+    query_sum,
+    query_all,
     outgoing,
     arrived,
     weights_in,
@@ -348,8 +438,12 @@
     z_recv,
     back_send,
     back_recv,
+    pair_send,
+    pair_recv,
+    query_send,
+    query_recv,
 ):
-    n_ctx, n_exp, chunks, n_x, n_z = sizes
+    n_ctx, n_exp, chunks, n_x, n_z, key_width, window, lags = sizes
     me = lax.axis_index("ctx")
     mine = lax.axis_index("exp")
     core = lax.rem(me, 2)
@@ -371,11 +465,49 @@
     def _(c):
         proj_copy(c).start()
 
-    greet((("ctx", n_ctx), ("exp", n_exp)))
+    chip = me // 2
+    meet(
+        [{"exp": lax.rem(mine + k, n_exp)} for k in range(1, n_exp)]
+        + [{"ctx": me + 1 - 2 * core}]
+        + [{"ctx": lax.rem(me + 2 * k, n_ctx)} for k in range(1, chips)]
+    )
+
+    ids, route = ids_ref[...], route_ref[...].astype(BF16).astype(F32)
+    tokens = ids.shape[1]
+    expert = lax.broadcasted_iota(jnp.int32, (n_exp, tokens), 0)
+    named = [expert == ids[k : k + 1] for k in range(ids.shape[0])]
+    chosen = sum(n.astype(F32) for n in named)
+    weight_of = sum(jnp.where(n, route[k : k + 1], 0.0) for k, n in enumerate(named))
+    before = lax.broadcasted_iota(jnp.int32, (tokens, tokens), 0) < lax.broadcasted_iota(
+        jnp.int32, (tokens, tokens), 1
+    )
+    rank = jnp.dot(chosen, before.astype(F32), preferred_element_type=F32).astype(jnp.int32)
+    rank = jnp.where(chosen > 0, rank, -1)
+    place = (
+        rank[:, None, :] == lax.broadcasted_iota(jnp.int32, (n_exp, capacity, tokens), 1)
+    ).astype(F32)
+    placing[...] = place.reshape(slots, tokens).astype(BF16)
+    slot_weights[...] = jnp.broadcast_to(
+        jnp.sum(place * weight_of[:, None, :], axis=2, keepdims=True), slot_weights.shape
+    ).astype(BF16)
+
+    def pair_copy():
+        return push(
+            query_ref.at[1 - core], query_in, pair_send.at[0], pair_recv.at[0], {"ctx": me + 1 - 2 * core}
+        )
+
+    def query_copy(there, source):
+        return push(
+            query_sum.at[there],
+            query_all.at[source],
+            query_send.at[there],
+            query_recv.at[source],
+            {"ctx": there * 2 + core},
+        )
 
     def weight_copy(there, source):
         return push(
-            slot_weights_ref.at[there],
+            slot_weights.at[there],
             weights_in.at[source],
             weight_send.at[there],
             weight_recv.at[source],
@@ -419,20 +551,25 @@
             slot_parts.at[there], returned.at[source], back_send.at[there], back_recv.at[source], {"exp": there}
         )
 
+    def send_slots(c):
+        @pl.loop(1, n_exp)
+        def _(k):
+            slot_copy(c, lax.rem(mine + k, n_exp), mine).start()
+
     @pl.loop(1, n_exp)
     def _(k):
         weight_copy(lax.rem(mine + k, n_exp), mine).start()
 
-    weights_in[mine] = slot_weights_ref[mine]
+    weights_in[mine] = slot_weights[mine]
 
     @pl.loop(0, chunks)
     def _(c):
-        placed = jnp.dot(placing_ref[...], stream_ref[:, columns(c)], preferred_element_type=F32)
+        placed = jnp.dot(placing[...], stream_ref[:, columns(c)], preferred_element_type=F32)
         outgoing[c] = placed.astype(BF16).reshape(n_exp, capacity, depth)
 
-        @pl.loop(1, n_exp)
-        def _(k):
-            slot_copy(c, lax.rem(mine + k, n_exp), mine).start()
+        @pl.when(c < window)
+        def _():
+            send_slots(c)
 
         arrived[c, mine] = outgoing[c, mine]
 
@@ -450,13 +587,19 @@
 
     through[...] = jnp.zeros(through.shape, F32)
 
-    @pl.loop(0, chunks + 3)
+    lag1, lag2, lag3 = lags
+
+    @pl.loop(0, chunks + lag3)
     def _(c):
         @pl.when(c < chunks)
         def _():
             @pl.loop(1, n_exp)
             def _(k):
                 slot_copy(c, mine, lax.rem(mine + k, n_exp)).wait_recv()
+
+            @pl.when(c + window < chunks)
+            def _():
+                send_slots(c + window)
 
             proj_copy(c).wait()
             rows = arrived[c].reshape(slots, depth)
@@ -465,9 +608,9 @@
             core_copy(c).start()
             through[...] += nt_dot(rows, proj[c])
 
-        @pl.when((c >= 1) & (c < chunks + 1))
-        def _():
-            d = c - 1
+        @pl.when((c >= lag1) & (c < chunks + lag1))
+        def _():
+            d = c - lag1
             core_copy(d).wait_recv()
             total = partial[d, core].astype(F32) + core_in[d].astype(F32)
             partial[d, core] = total.astype(BF16)
@@ -477,9 +620,9 @@
             def _(k):
                 x_copy(d, lax.rem(x_at + k, n_x), x_at).start()
 
-        @pl.when((c >= 2) & (c < chunks + 2))
-        def _():
-            d = c - 2
+        @pl.when((c >= lag2) & (c < chunks + lag2))
+        def _():
+            d = c - lag2
 
             @pl.loop(1, n_x)
             def _(k):
@@ -491,12 +634,25 @@
             z_part[d] = total.astype(BF16)
             z_copy(d).start()
 
-        @pl.when(c >= 3)
-        def _():
-            d = c - 3
+        @pl.when(c >= lag3)
+        def _():
+            d = c - lag3
             z_copy(d).wait_recv()
             total = z_part[d, z_at].astype(F32) + z_in[d].astype(F32)
             down_out[:, columns(d)] = total.astype(BF16)
+
+        @pl.when(c == 1)
+        def _():
+            pair_copy().start()
+
+        @pl.when(c == chunks // 2)
+        def _():
+            pair_copy().wait_recv()
+            query_sum[...] = (query_ref[core].astype(F32) + query_in[...].astype(F32)).astype(BF16)
+
+            @pl.loop(chip + 1, chips)
+            def _(q):
+                query_copy(q, chip).start()
 
         @pl.when(c == chunks - 1)
         def _():
@@ -510,6 +666,17 @@
                 back_copy(lax.rem(mine + k, n_exp), mine).start()
 
             returned[mine] = slot_parts[mine]
+
+    def add(p, so_far):
+        query_copy(chip, p).wait_recv()
+        return so_far + query_all[p].astype(F32)
+
+    query_total = lax.fori_loop(0, chip, add, query_sum[chip].astype(F32))
+    query_rows = query_out.shape[0]
+    heads = query_out.shape[1] // key_width
+    query_out[...] = jnp.concatenate(
+        [query_total[h * query_rows : (h + 1) * query_rows, :key_width] for h in range(heads)], axis=1
+    ).astype(BF16)
 
     @pl.loop(1, n_exp)
     def _(k):
@@ -518,6 +685,20 @@
         back_copy(there, mine).wait_send()
         weight_copy(there, mine).wait_send()
 
+    moved = jnp.sum(
+        placing[...].astype(F32).reshape(n_exp, capacity, tokens) * returned[...], axis=1
+    )
+    for k in range(ids_ref.shape[0]):
+        weight_out[k : k + 1] = jnp.sum(
+            jnp.where(expert == ids_ref[k : k + 1], moved, 0.0), axis=0, keepdims=True
+        )
+
+    pair_copy().wait_send()
+
+    @pl.loop(chip + 1, chips)
+    def _(q):
+        query_copy(q, chip).wait_send()
+
     @pl.loop(0, chunks)
     def _(c):
         @pl.loop(1, n_exp)
@@ -533,10 +714,11 @@
         z_copy(c).wait_send()
 
 
-def experts(stream_total, placing, slot_weights, acts, proj):
+def experts(stream_total, query_parts, ids, route, acts, proj, key_width, query_rows):
     n_ctx, n_exp = lax.axis_size("ctx"), lax.axis_size("exp")
     slots, inner = acts.shape
-    width = stream_total.shape[1]
+    tokens, width = stream_total.shape
+    top_count = ids.shape[1]
     capacity = slots // n_exp
     chunks = 10
     n_z = 2
@@ -544,20 +726,28 @@
     depth = width // chunks
     share = inner // n_ctx
     chips = n_ctx // 2
-    wide_weights = jnp.broadcast_to(slot_weights[:, None], (slots, LANES)).reshape(n_exp, capacity, LANES)
+    per, wide = query_parts.shape[2:]
     vmem = pl.BlockSpec(memory_space=pltpu.VMEM)
     dma = pltpu.SemaphoreType.DMA
+    sizes = (n_ctx, n_exp, chunks, n_x, n_z, key_width, 2, (1, 2, 3))
     return pl.pallas_call(
-        functools.partial(expert_kernel, (n_ctx, n_exp, chunks, n_x, n_z)),
+        functools.partial(expert_kernel, sizes),
         out_shape=(
             jax.ShapeDtypeStruct((slots, inner), BF16),
             jax.ShapeDtypeStruct((share, width), BF16),
-            jax.ShapeDtypeStruct((n_exp, capacity, LANES), F32),
+            jax.ShapeDtypeStruct((top_count, tokens), F32),
+            jax.ShapeDtypeStruct((query_rows, per // query_rows * key_width), BF16),
         ),
-        in_specs=[vmem, vmem, vmem, vmem, pl.BlockSpec(memory_space=pl.ANY)],
-        out_specs=(vmem, vmem, vmem),
+        in_specs=[vmem, vmem, vmem, vmem, vmem, pl.BlockSpec(memory_space=pl.ANY)],
+        out_specs=(vmem, vmem, vmem, vmem),
         scratch_shapes=[
             pltpu.VMEM((chunks, inner, depth), BF16),
+            pltpu.VMEM((slots, tokens), BF16),
+            pltpu.VMEM((n_exp, capacity, LANES), BF16),
+            pltpu.VMEM((n_exp, capacity, LANES), F32),
+            pltpu.VMEM((chips, per, wide), BF16),
+            pltpu.VMEM((chips, per, wide), BF16),
+            pltpu.VMEM((chips, per, wide), BF16),
             pltpu.VMEM((chunks, n_exp, capacity, depth), BF16),
             pltpu.VMEM((chunks, n_exp, capacity, depth), BF16),
             pltpu.VMEM((n_exp, capacity, LANES), BF16),
@@ -582,11 +772,15 @@
             dma((chunks,)),
             dma((n_exp,)),
             dma((n_exp,)),
+            dma((1,)),
+            dma((1,)),
+            dma((chips,)),
+            dma((chips,)),
         ],
         compiler_params=pltpu.CompilerParams(
-            collective_id=1, has_side_effects=True, vmem_limit_bytes=60 * 2**20
+            collective_id=1, has_side_effects=True, vmem_limit_bytes=61 * 2**20
         ),
-    )(stream_total, placing, wide_weights, acts, proj)
+    )(stream_total, query_parts, ids.T, route.T, acts, proj)
 
 
 def body(
@@ -602,42 +796,20 @@
     expert_acts,
     down_proj,
 ):
-    query_grad, key_rows = attention(queries, latents, out_grad)
-    norm_grad = lax.dot_general(
-        key_rows, latent_proj, (((1,), (1,)), ((), ())), preferred_element_type=jnp.float32
+    stream_total, query_parts = attention(
+        queries, latents, out_grad, hidden_rows, norm_gain, latent_proj, stream_grad
     )
-    row_values = hidden_rows.astype(jnp.float32)
-    inverse = lax.rsqrt(jnp.mean(row_values * row_values, axis=-1, keepdims=True) + EPSILON)
-    gained = norm_gain * norm_grad
-    through_norm = inverse * gained - row_values * (inverse * inverse * inverse) * jnp.mean(
-        row_values * gained, axis=-1, keepdims=True
+    act_grad, down_share, weight_grad, query_grad = experts(
+        stream_total,
+        query_parts,
+        expert_ids,
+        route_weights,
+        expert_acts[0],
+        down_proj[0],
+        latents.shape[1],
+        queries.shape[0],
     )
-    stream_total = (stream_grad.astype(jnp.float32) + through_norm).astype(jnp.bfloat16)
-    expert_count = lax.axis_size("exp")
-    slot_count = expert_acts.shape[1]
-    capacity = slot_count // expert_count
-    local_rows = expert_ids.shape[0]
-    top_count = expert_ids.shape[1]
-    flat_ids = expert_ids.reshape(-1)
-    chosen = (flat_ids[:, None] == jnp.arange(expert_count, dtype=jnp.int32)[None, :]).astype(
-        jnp.int32
-    )
-    earlier = jnp.cumsum(chosen, axis=0) - chosen
-    slot_of = flat_ids * capacity + jnp.sum(earlier * chosen, axis=1)
-    select = (slot_of[:, None] == jnp.arange(slot_count, dtype=jnp.int32)[None, :]).astype(
-        jnp.float32
-    )
-    select = select.reshape(local_rows, top_count, slot_count)
-    placing = jnp.sum(select, axis=1).astype(jnp.bfloat16)
-    rounded_weights = lax.optimization_barrier(route_weights.astype(jnp.bfloat16)).astype(
-        jnp.float32
-    )
-    weight_slots = jnp.einsum("tks,tk->s", select, rounded_weights).astype(jnp.bfloat16)
-    act_grad, down_share, returned = experts(
-        stream_total, placing.T, weight_slots, expert_acts[0], down_proj[0]
-    )
-    weight_grad = jnp.einsum("tks,s->tk", select, returned[:, :, 0].reshape(slot_count))
-    return (query_grad, stream_total, act_grad[None], down_share[None], weight_grad)
+    return (query_grad, stream_total, act_grad[None], down_share[None], weight_grad.T)
 
 
 def solution(mesh):

time: 212 us -> 178 us (0.84)
  Pallas kernels: 186 us -> 171 us
  local copies, waits for them, and re-layouts: 14.3 us -> 5.79 us
  matrix products: 5.43 us -> 0 us
  other arithmetic: 2.79 us -> 0 us
    pallas_call x1, Pallas kernels: 70.5 us -> 57.2 us  [attention(): pl.pallas_call(functools.partial(attention_kernel, sizes), out_shape=(jax...]
    dot_general x3 -> x0, matrix products: 5.43 us -> none  [the longest x1 4.34 us: body(): lax.dot_general(key_rows, latent_proj, (((1,), (1,)), ((), ())), preferre...]
    reshape x3 -> x0, local copies, waits for them, and re-layouts: 3.63 us -> none  [the longest x1 1.64 us: attention(): query_grad[:, :key_width].reshape(query_rows, heads * key_width)]
    unnamed x14 -> x13, local copies, waits for them, and re-layouts: 6.43 us -> 5.79 us
where the time goes in v3:
time: 178 us; the launch traced here: 177 us
  Pallas kernels  171 us (96%)
  local copies, waits for them, and re-layouts  5.79 us (3%)
    pallas_call x1, Pallas kernels, experts(): pl.pallas_call(functools.partial(expert_kernel, sizes), out_shape=(jax.Sh...  114 us
    pallas_call x1, Pallas kernels, attention(): pl.pallas_call(functools.partial(attention_kernel, sizes), out_shape=(jax...  57.2 us
    unnamed x13, local copies, waits for them, and re-layouts  5.79 us

profile of v3, /device:TPU:0, one launch (start us, length us, event | category | flops | bytes accessed | tf_op | source)
XLA Modules:
  0.0 177.3 jit_solution(2605091616146426378)
XLA Ops:
  0.6 57.2 %shard_map.146 = (bf16[128,5120]{1,0:T(8,128)(2,1)}, bf16[2,8,64,640]{3,2,1,0:T(8,128)(2,1)}) custom-call(bf16[8,4608]{1,0:T(8,128)(2,1)} %queries_ref.1, bf16[8,4096]{1,0:T(8,128)(2,1)} %out_grad_ref.1, bf16[576,1024]{1,0:T(8,128)(2,1)} %bitcast.12, f32[1,5120]{1,0:T(1,128)} %bitcast.16, bf16[128,5120]{1,0:T(8,128)(2,1)} %hidden_hbm.1, ...), custom_call_target="tpu_custom_call" | custom-call | tf_op jit(solution)/shard_map/pallas_call | solution.py:355
  57.8 0.0 copy-start
  57.8 113.7 %shard_map.147 = (bf16[512,768]{1,0:T(8,128)(2,1)}, bf16[48,5120]{1,0:T(8,128)(2,1)}, f32[2,128]{1,0:T(2,128)}, bf16[8,4608]{1,0:T(8,128)(2,1)}) custom-call(bf16[128,5120]{1,0:T(8,128)(2,1)} %get-tuple-element.23.stream_ref, bf16[2,8,64,640]{3,2,1,0:T(8,128)(2,1)} %get-tuple-element.12.query_ref, s32[2,128]{1,0:T(2,128)} %bitcast.17, f32[2,128]{1,0:T(2,128)} %bitcast.18, ...), custom_call_target="tpu_custom_call" | custom-call | tf_op jit(solution)/shard_map/pallas_call | solution.py:733
  171.5 1.5 copy.21
  173.1 0.0 copy-done
  173.1 0.0 copy-start.1
  173.1 1.1 copy.22
  174.1 0.5 copy-done.1
  174.7 0.0 copy-start.2
  174.7 0.0 copy-start.3
  174.7 0.9 copy.23
  175.5 0.4 copy-done.2
  176.0 0.8 copy.24
  176.8 0.0 copy-done.3
  176.8 0.6 copy.25
Async XLA Ops:
  57.8 115.2 %copy-start = (bf16[128,5120]{1,0:T(8,128)(2,1)S(1)}, bf16[128,5120]{1,0:T(8,128)(2,1)}, u32[]{:S(2)}) copy-start(bf16[128,5120]{1,0:T(8,128)(2,1)} %get-tuple-element.23.stream_ref) | copy-start | bytes 3932164
  173.1 1.6 copy-start.1
  174.7 1.3 copy-start.2
  174.7 2.1 %copy-start.3 = (f32[2,128]{1,0:T(2,128)S(1)}, f32[2,128]{1,0:T(2,128)}, u32[]{:S(2)}) copy-start(f32[2,128]{1,0:T(2,128)} %get-tuple-element.16) | copy-start | bytes 3076

commit v4 on v3

--- a/solution.py
+++ b/solution.py
@@ -409,6 +409,8 @@
     query_out,
     proj,
     placing,
+    peer_placing,
+    peer_rows,
     slot_weights,
     returned,
     query_in,
@@ -426,6 +428,10 @@
     z_in,
     slot_parts,
     proj_sem,
+    place_send,
+    place_recv,
+    peer_send,
+    peer_recv,
     slot_send,
     slot_recv,
     weight_send,
@@ -466,6 +472,13 @@
         proj_copy(c).start()
 
     chip = me // 2
+    l_at, y_at = lax.rem(mine, 2), mine // 2
+    n_y = n_exp // 2
+    partner = mine + 1 - 2 * l_at
+
+    def turned_index(e):
+        return lax.rem(e, 2) * n_y + e // 2
+
     meet(
         [{"exp": lax.rem(mine + k, n_exp)} for k in range(1, n_exp)]
         + [{"ctx": me + 1 - 2 * core}]
@@ -474,7 +487,8 @@
 
     ids, route = ids_ref[...], route_ref[...].astype(BF16).astype(F32)
     tokens = ids.shape[1]
-    expert = lax.broadcasted_iota(jnp.int32, (n_exp, tokens), 0)
+    row = lax.broadcasted_iota(jnp.int32, (n_exp, tokens), 0)
+    expert = row % n_y * 2 + row // n_y
     named = [expert == ids[k : k + 1] for k in range(ids.shape[0])]
     chosen = sum(n.astype(F32) for n in named)
     weight_of = sum(jnp.where(n, route[k : k + 1], 0.0) for k, n in enumerate(named))
@@ -486,7 +500,7 @@
     place = (
         rank[:, None, :] == lax.broadcasted_iota(jnp.int32, (n_exp, capacity, tokens), 1)
     ).astype(F32)
-    placing[...] = place.reshape(slots, tokens).astype(BF16)
+    placing[...] = place.reshape(2, slots // 2, tokens).astype(BF16)
     slot_weights[...] = jnp.broadcast_to(
         jnp.sum(place * weight_of[:, None, :], axis=2, keepdims=True), slot_weights.shape
     ).astype(BF16)
@@ -507,20 +521,20 @@
 
     def weight_copy(there, source):
         return push(
-            slot_weights.at[there],
+            slot_weights.at[turned_index(there)],
             weights_in.at[source],
             weight_send.at[there],
             weight_recv.at[source],
             {"exp": there},
         )
 
-    def slot_copy(c, there, source):
-        return push(
-            outgoing.at[c, there],
+    def slot_copy(c, k, there, source):
+        return push(
+            outgoing.at[c, k, there],
             arrived.at[c, source],
-            slot_send.at[c, there],
+            slot_send.at[c, k, there],
             slot_recv.at[c, source],
-            {"exp": there},
+            {"exp": there * 2 + l_at},
         )
 
     def core_copy(c):
@@ -548,30 +562,52 @@
 
     def back_copy(there, source):
         return push(
-            slot_parts.at[there], returned.at[source], back_send.at[there], back_recv.at[source], {"exp": there}
-        )
+            slot_parts.at[there], returned.at[turned_index(source)], back_send.at[there], back_recv.at[source], {"exp": there}
+        )
+
+    def place_copy():
+        return push(
+            placing.at[1 - l_at], peer_placing, place_send.at[0], place_recv.at[0], {"exp": partner}
+        )
+
+    def rows_copy(c):
+        return push(
+            stream_ref.at[:, columns(c)], peer_rows.at[c], peer_send.at[c], peer_recv.at[c], {"exp": partner}
+        )
+
+    def put_out(c, k, rows, place, source):
+        placed = jnp.dot(place, rows, preferred_element_type=F32)
+        outgoing[c, k] = placed.astype(BF16).reshape(n_y, capacity, depth)
+
+        @pl.loop(1, n_y)
+        def _(n):
+            slot_copy(c, k, lax.rem(y_at + n, n_y), source).start()
+
+        arrived[c, source] = outgoing[c, k, y_at]
 
     def send_slots(c):
-        @pl.loop(1, n_exp)
-        def _(k):
-            slot_copy(c, lax.rem(mine + k, n_exp), mine).start()
+        put_out(c, 0, stream_ref[:, columns(c)], placing[l_at], mine)
+        rows_copy(c).wait_recv()
+        put_out(c, 1, peer_rows[c], peer_placing[...], partner)
+
+        @pl.when(c + ahead < chunks)
+        def _():
+            rows_copy(c + ahead).start()
+
+    ahead = window + 2
+    place_copy().start()
+    for c in range(ahead):
+        rows_copy(c).start()
 
     @pl.loop(1, n_exp)
     def _(k):
         weight_copy(lax.rem(mine + k, n_exp), mine).start()
 
-    weights_in[mine] = slot_weights[mine]
-
-    @pl.loop(0, chunks)
-    def _(c):
-        placed = jnp.dot(placing[...], stream_ref[:, columns(c)], preferred_element_type=F32)
-        outgoing[c] = placed.astype(BF16).reshape(n_exp, capacity, depth)
-
-        @pl.when(c < window)
-        def _():
-            send_slots(c)
-
-        arrived[c, mine] = outgoing[c, mine]
+    weights_in[mine] = slot_weights[turned_index(mine)]
+
+    place_copy().wait_recv()
+    for c in range(window):
+        send_slots(c)
 
     @pl.loop(1, n_exp)
     def _(k):
@@ -593,13 +629,10 @@
     def _(c):
         @pl.when(c < chunks)
         def _():
-            @pl.loop(1, n_exp)
-            def _(k):
-                slot_copy(c, mine, lax.rem(mine + k, n_exp)).wait_recv()
-
-            @pl.when(c + window < chunks)
-            def _():
-                send_slots(c + window)
+            @pl.loop(1, n_y)
+            def _(n):
+                for k in range(2):
+                    slot_copy(c, 0, y_at, lax.rem(y_at + n, n_y) * 2 + k).wait_recv()
 
             proj_copy(c).wait()
             rows = arrived[c].reshape(slots, depth)
@@ -641,6 +674,10 @@
             total = z_part[d, z_at].astype(F32) + z_in[d].astype(F32)
             down_out[:, columns(d)] = total.astype(BF16)
 
+        @pl.when(c + window < chunks)
+        def _():
+            send_slots(c + window)
+
         @pl.when(c == 1)
         def _():
             pair_copy().start()
@@ -665,7 +702,7 @@
             def _(k):
                 back_copy(lax.rem(mine + k, n_exp), mine).start()
 
-            returned[mine] = slot_parts[mine]
+            returned[turned_index(mine)] = slot_parts[mine]
 
     def add(p, so_far):
         query_copy(chip, p).wait_recv()
@@ -694,6 +731,7 @@
         )
 
     pair_copy().wait_send()
+    place_copy().wait_send()
 
     @pl.loop(chip + 1, chips)
     def _(q):
@@ -701,9 +739,12 @@
 
     @pl.loop(0, chunks)
     def _(c):
-        @pl.loop(1, n_exp)
-        def _(k):
-            slot_copy(c, lax.rem(mine + k, n_exp), mine).wait_send()
+        rows_copy(c).wait_send()
+
+        @pl.loop(1, n_y)
+        def _(n):
+            for k in range(2):
+                slot_copy(c, k, lax.rem(y_at + n, n_y), mine).wait_send()
 
         core_copy(c).wait_send()
 
@@ -729,7 +770,7 @@
     per, wide = query_parts.shape[2:]
     vmem = pl.BlockSpec(memory_space=pltpu.VMEM)
     dma = pltpu.SemaphoreType.DMA
-    sizes = (n_ctx, n_exp, chunks, n_x, n_z, key_width, 2, (1, 2, 3))
+    sizes = (n_ctx, n_exp, chunks, n_x, n_z, key_width, 3, (1, 3, 5))
     return pl.pallas_call(
         functools.partial(expert_kernel, sizes),
         out_shape=(
@@ -742,13 +783,15 @@
         out_specs=(vmem, vmem, vmem, vmem),
         scratch_shapes=[
             pltpu.VMEM((chunks, inner, depth), BF16),
-            pltpu.VMEM((slots, tokens), BF16),
+            pltpu.VMEM((2, slots // 2, tokens), BF16),
+            pltpu.VMEM((slots // 2, tokens), BF16),
+            pltpu.VMEM((chunks, tokens, depth), BF16),
             pltpu.VMEM((n_exp, capacity, LANES), BF16),
             pltpu.VMEM((n_exp, capacity, LANES), F32),
             pltpu.VMEM((chips, per, wide), BF16),
             pltpu.VMEM((chips, per, wide), BF16),
             pltpu.VMEM((chips, per, wide), BF16),
-            pltpu.VMEM((chunks, n_exp, capacity, depth), BF16),
+            pltpu.VMEM((chunks, 2, n_exp // 2, capacity, depth), BF16),
             pltpu.VMEM((chunks, n_exp, capacity, depth), BF16),
             pltpu.VMEM((n_exp, capacity, LANES), BF16),
             pltpu.VMEM((inner, slots), BF16),
@@ -760,7 +803,11 @@
             pltpu.VMEM((chunks, share, depth), BF16),
             pltpu.VMEM((n_exp, capacity, LANES), F32),
             dma((chunks,)),
-            dma((chunks, n_exp)),
+            dma((1,)),
+            dma((1,)),
+            dma((chunks,)),
+            dma((chunks,)),
+            dma((chunks, 2, n_exp // 2)),
             dma((chunks, n_exp)),
             dma((n_exp,)),
             dma((n_exp,)),

time: 178 us -> 158 us (0.89)
  Pallas kernels: 171 us -> 151 us
    pallas_call x1, Pallas kernels: 114 us -> 94.1 us  [experts(): pl.pallas_call(functools.partial(expert_kernel, sizes), out_shape=(jax.Sh...]
where the time goes in v4:
time: 158 us
  Pallas kernels  151 us (96%)
  local copies, waits for them, and re-layouts  5.79 us (4%)
    pallas_call x1, Pallas kernels, experts(): pl.pallas_call(functools.partial(expert_kernel, sizes), out_shape=(jax.Sh...  94.1 us
    pallas_call x1, Pallas kernels, attention(): pl.pallas_call(functools.partial(attention_kernel, sizes), out_shape=(jax...  57.2 us
    unnamed x13, local copies, waits for them, and re-layouts  5.79 us

profile of v4, /device:TPU:0, one launch (start us, length us, event | category | flops | bytes accessed | tf_op | source)
XLA Modules:
  0.0 157.7 jit_solution(5234301910293901536)
XLA Ops:
  0.6 57.2 %shard_map.146 = (bf16[128,5120]{1,0:T(8,128)(2,1)}, bf16[2,8,64,640]{3,2,1,0:T(8,128)(2,1)}) custom-call(bf16[8,4608]{1,0:T(8,128)(2,1)} %queries_ref.1, bf16[8,4096]{1,0:T(8,128)(2,1)} %out_grad_ref.1, bf16[576,1024]{1,0:T(8,128)(2,1)} %bitcast.12, f32[1,5120]{1,0:T(1,128)} %bitcast.16, bf16[128,5120]{1,0:T(8,128)(2,1)} %hidden_hbm.1, ...), custom_call_target="tpu_custom_call" | custom-call | tf_op jit(solution)/shard_map/pallas_call | solution.py:355
  57.8 0.0 copy-start
  57.8 94.1 %shard_map.147 = (bf16[512,768]{1,0:T(8,128)(2,1)}, bf16[48,5120]{1,0:T(8,128)(2,1)}, f32[2,128]{1,0:T(2,128)}, bf16[8,4608]{1,0:T(8,128)(2,1)}) custom-call(bf16[128,5120]{1,0:T(8,128)(2,1)} %get-tuple-element.23.stream_ref, bf16[2,8,64,640]{3,2,1,0:T(8,128)(2,1)} %get-tuple-element.12.query_ref, s32[2,128]{1,0:T(2,128)} %bitcast.17, f32[2,128]{1,0:T(2,128)} %bitcast.18, ...), custom_call_target="tpu_custom_call" | custom-call | tf_op jit(solution)/shard_map/pallas_call | solution.py:774
  152.0 1.5 copy.21
  153.5 0.0 copy-done
  153.5 0.0 copy-start.1
  153.5 1.1 copy.22
  154.5 0.5 copy-done.1
  155.1 0.0 copy-start.2
  155.1 0.0 copy-start.3
  155.1 0.9 copy.23
  156.0 0.4 copy-done.2
  156.4 0.8 copy.24
  157.2 0.0 copy-done.3
  157.2 0.6 copy.25
Async XLA Ops:
  57.8 95.7 %copy-start = (bf16[128,5120]{1,0:T(8,128)(2,1)S(1)}, bf16[128,5120]{1,0:T(8,128)(2,1)}, u32[]{:S(2)}) copy-start(bf16[128,5120]{1,0:T(8,128)(2,1)} %get-tuple-element.23.stream_ref) | copy-start | bytes 3932164
  153.5 1.6 %copy-start.1 = (bf16[512,768]{1,0:T(8,128)(2,1)S(1)}, bf16[512,768]{1,0:T(8,128)(2,1)}, u32[]{:S(2)}) copy-start(bf16[512,768]{1,0:T(8,128)(2,1)} %get-tuple-element.14) | copy-start | bytes 2359300
  155.1 1.3 copy-start.2
  155.1 2.1 %copy-start.3 = (f32[2,128]{1,0:T(2,128)S(1)}, f32[2,128]{1,0:T(2,128)}, u32[]{:S(2)}) copy-start(f32[2,128]{1,0:T(2,128)} %get-tuple-element.16) | copy-start | bytes 3076

commit v5 on v4

--- a/solution.py
+++ b/solution.py
@@ -7,6 +7,7 @@
 from jax.sharding import PartitionSpec as P
 
 EPSILON = 1e-06
+LEAD = 2
 NEG_LARGE = -1e30
 MESH = pl.DeviceIdType.MESH
 F32 = jnp.float32
@@ -48,15 +49,10 @@
     pl.semaphore_wait(barrier, total)
 
 
-def meet(peers):
-    barrier = pltpu.get_barrier_semaphore()
-    for where in peers:
-        pl.semaphore_signal(barrier, inc=1, device_id=where, device_id_type=MESH)
-    pl.semaphore_wait(barrier, len(peers))
-
-
-def attention_kernel(
+def attention_part(
     sizes,
+    idle,
+    ready,
     queries_ref,
     out_grad_ref,
     latents_t_ref,
@@ -86,7 +82,7 @@
     key_send,
     key_recv,
 ):
-    n_ctx, n_exp, key_width, value_width, query_rows, heads = sizes
+    n_ctx, n_exp, key_width, value_width, query_rows, heads, chunks = sizes
     wide = padded(key_width)
     me = lax.axis_index("ctx")
     mine = lax.axis_index("exp")
@@ -105,9 +101,6 @@
     hidden_load = pltpu.make_async_copy(hidden_hbm, hidden, load_sem.at[0])
     proj_load = pltpu.make_async_copy(proj_t_hbm, proj_t.at[:key_width], load_sem.at[1])
     stream_load = pltpu.make_async_copy(stream_hbm, stream, load_sem.at[2])
-    for copy in (hidden_load, proj_load, stream_load):
-        copy.start()
-
     query_values = queries_ref[...].astype(F32)
     grad_values = out_grad_ref[...].astype(F32)
     rows_all[me, :, :key_width] = jnp.concatenate(
@@ -118,8 +111,6 @@
         [grad_values[:, h * value_width : (h + 1) * value_width] for h in range(heads)], axis=0
     ).astype(BF16)
 
-    greet((("ctx", n_ctx), ("exp", n_exp)))
-
     def rows_copy(there, source):
         return push(
             rows_all.at[source],
@@ -145,6 +136,9 @@
     @pl.when(core == 1)
     def _():
         pass_copy(me).start()
+
+    for copy in (hidden_load, proj_load, stream_load):
+        copy.start()
 
     @pl.loop(0, me)
     def _(i):
@@ -162,6 +156,8 @@
         at = pl.ds(pl.multiple_of(g * cols, cols), cols)
         weights[:, at] = jnp.zeros((key_count, cols), F32)
         grads[:, at] = jnp.zeros((key_count, cols), F32)
+
+    idle()
 
     def compute(g):
         for k in range(n_groups // 2):
@@ -301,7 +297,7 @@
     aligned = jnp.sum(key_rows.astype(F32) * pulled, axis=1, keepdims=True)
     back = inverse * inverse * inverse * aligned
     stream_load.wait()
-    depth = 512
+    depth = width // chunks
 
     @pl.loop(0, width // depth)
     def _(c):
@@ -309,6 +305,7 @@
         norm_grad = jnp.dot(key_rows, proj_t[:, at], preferred_element_type=F32)
         through_norm = inverse * (gain_ref[:, at] * norm_grad) - hidden[:, at].astype(F32) * back
         stream_out[:, at] = (stream[:, at].astype(F32) + through_norm).astype(BF16)
+        ready(c)
 
     @pl.loop(0, me // 2)
     def _(i):
@@ -337,70 +334,41 @@
             key_copy(s, mine).wait_send()
 
 
-def attention(queries, latents, out_grad, hidden_rows, norm_gain, latent_proj, stream_grad):
-    key_count, key_width = latents.shape
-    query_rows = queries.shape[0]
-    heads = queries.shape[1] // key_width
-    value_width = out_grad.shape[1] // heads
-    per = query_rows * heads
-    wide = padded(key_width)
-    n_ctx, n_exp = lax.axis_size("ctx"), lax.axis_size("exp")
-    piece = key_count // n_exp
-    total_rows = n_ctx * per
-    token_rows, width = hidden_rows.shape
-    sizes = (n_ctx, n_exp, key_width, value_width, query_rows, heads)
-    vmem = pl.BlockSpec(memory_space=pltpu.VMEM)
-    hbm = pl.BlockSpec(memory_space=pl.ANY)
-    dma = pltpu.SemaphoreType.DMA
-    return pl.pallas_call(
-        functools.partial(attention_kernel, sizes),
-        out_shape=(
-            jax.ShapeDtypeStruct((token_rows, width), BF16),
-            jax.ShapeDtypeStruct((2, n_ctx // 2, per, wide), BF16),
-        ),
-        in_specs=[vmem, vmem, vmem, vmem, hbm, hbm, hbm],
-        out_specs=(vmem, vmem),
-        scratch_shapes=[
-            pltpu.VMEM((n_ctx, per, wide + value_width), BF16),
-            pltpu.VMEM((n_ctx, 3, total_rows // LANES, LANES), F32),
-            pltpu.VMEM((key_count, wide), BF16),
-            pltpu.VMEM((key_count, total_rows), F32),
-            pltpu.VMEM((key_count, total_rows), F32),
-            pltpu.VMEM((key_count, total_rows), BF16),
-            pltpu.VMEM((n_exp, piece, wide), BF16),
-            pltpu.VMEM((n_exp, piece, wide), BF16),
-            pltpu.VMEM((token_rows, width), BF16),
-            pltpu.VMEM((token_rows, width), BF16),
-            pltpu.VMEM((wide, width), BF16),
-            dma((3,)),
-            dma((n_ctx,)),
-            dma((n_ctx,)),
-            dma((n_ctx,)),
-            dma((n_ctx,)),
-            dma((n_ctx,)),
-            dma((n_exp,)),
-            dma((n_exp,)),
-        ],
-        compiler_params=pltpu.CompilerParams(
-            collective_id=0, has_side_effects=True, vmem_limit_bytes=58 * 2**20
-        ),
-    )(
-        queries,
-        out_grad,
-        latents.T,
-        norm_gain.reshape(1, width),
-        hidden_rows,
-        stream_grad,
-        latent_proj.T,
+def expert_of_row(n_exp, tokens):
+    row = lax.broadcasted_iota(jnp.int32, (n_exp, tokens), 0)
+    return row % (n_exp // 2) * 2 + row // (n_exp // 2)
+
+
+def slot_tables(ids_ref, route_ref, placing, slot_weights):
+    n_exp, capacity = slot_weights.shape[:2]
+    ids, route = ids_ref[...], route_ref[...].astype(BF16).astype(F32)
+    tokens = ids.shape[1]
+    expert = expert_of_row(n_exp, tokens)
+    named = [expert == ids[k : k + 1] for k in range(ids.shape[0])]
+    chosen = sum(n.astype(F32) for n in named)
+    weight_of = sum(jnp.where(n, route[k : k + 1], 0.0) for k, n in enumerate(named))
+    before = lax.broadcasted_iota(jnp.int32, (tokens, tokens), 0) < lax.broadcasted_iota(
+        jnp.int32, (tokens, tokens), 1
     )
-
-
-def expert_kernel(
+    rank = jnp.dot(chosen, before.astype(F32), preferred_element_type=F32).astype(jnp.int32)
+    rank = jnp.where(chosen > 0, rank, -1)
+    place = (
+        rank[:, None, :] == lax.broadcasted_iota(jnp.int32, (n_exp, capacity, tokens), 1)
+    ).astype(F32)
+    placing[...] = place.reshape(placing.shape).astype(BF16)
+    slot_weights[...] = jnp.broadcast_to(
+        jnp.sum(place * weight_of[:, None, :], axis=2, keepdims=True), slot_weights.shape
+    ).astype(BF16)
+
+
+def expert_part(
     sizes,
+    place_copy,
+    rows_copy,
+    weight_copy,
     stream_ref,
     query_ref,
     ids_ref,
-    route_ref,
     acts_ref,
     proj_hbm,
     act_out,
@@ -467,10 +435,6 @@
     def proj_copy(c):
         return pltpu.make_async_copy(proj_hbm.at[:, columns(c)], proj.at[c], proj_sem.at[c])
 
-    @pl.loop(0, chunks)
-    def _(c):
-        proj_copy(c).start()
-
     chip = me // 2
     l_at, y_at = lax.rem(mine, 2), mine // 2
     n_y = n_exp // 2
@@ -479,31 +443,8 @@
     def turned_index(e):
         return lax.rem(e, 2) * n_y + e // 2
 
-    meet(
-        [{"exp": lax.rem(mine + k, n_exp)} for k in range(1, n_exp)]
-        + [{"ctx": me + 1 - 2 * core}]
-        + [{"ctx": lax.rem(me + 2 * k, n_ctx)} for k in range(1, chips)]
-    )
-
-    ids, route = ids_ref[...], route_ref[...].astype(BF16).astype(F32)
-    tokens = ids.shape[1]
-    row = lax.broadcasted_iota(jnp.int32, (n_exp, tokens), 0)
-    expert = row % n_y * 2 + row // n_y
-    named = [expert == ids[k : k + 1] for k in range(ids.shape[0])]
-    chosen = sum(n.astype(F32) for n in named)
-    weight_of = sum(jnp.where(n, route[k : k + 1], 0.0) for k, n in enumerate(named))
-    before = lax.broadcasted_iota(jnp.int32, (tokens, tokens), 0) < lax.broadcasted_iota(
-        jnp.int32, (tokens, tokens), 1
-    )
-    rank = jnp.dot(chosen, before.astype(F32), preferred_element_type=F32).astype(jnp.int32)
-    rank = jnp.where(chosen > 0, rank, -1)
-    place = (
-        rank[:, None, :] == lax.broadcasted_iota(jnp.int32, (n_exp, capacity, tokens), 1)
-    ).astype(F32)
-    placing[...] = place.reshape(2, slots // 2, tokens).astype(BF16)
-    slot_weights[...] = jnp.broadcast_to(
-        jnp.sum(place * weight_of[:, None, :], axis=2, keepdims=True), slot_weights.shape
-    ).astype(BF16)
+    tokens = ids_ref.shape[1]
+    expert = expert_of_row(n_exp, tokens)
 
     def pair_copy():
         return push(
@@ -519,15 +460,6 @@
             {"ctx": there * 2 + core},
         )
 
-    def weight_copy(there, source):
-        return push(
-            slot_weights.at[turned_index(there)],
-            weights_in.at[source],
-            weight_send.at[there],
-            weight_recv.at[source],
-            {"exp": there},
-        )
-
     def slot_copy(c, k, there, source):
         return push(
             outgoing.at[c, k, there],
@@ -565,16 +497,6 @@
             slot_parts.at[there], returned.at[turned_index(source)], back_send.at[there], back_recv.at[source], {"exp": there}
         )
 
-    def place_copy():
-        return push(
-            placing.at[1 - l_at], peer_placing, place_send.at[0], place_recv.at[0], {"exp": partner}
-        )
-
-    def rows_copy(c):
-        return push(
-            stream_ref.at[:, columns(c)], peer_rows.at[c], peer_send.at[c], peer_recv.at[c], {"exp": partner}
-        )
-
     def put_out(c, k, rows, place, source):
         placed = jnp.dot(place, rows, preferred_element_type=F32)
         outgoing[c, k] = placed.astype(BF16).reshape(n_y, capacity, depth)
@@ -594,20 +516,14 @@
         def _():
             rows_copy(c + ahead).start()
 
-    ahead = window + 2
-    place_copy().start()
-    for c in range(ahead):
-        rows_copy(c).start()
-
-    @pl.loop(1, n_exp)
-    def _(k):
-        weight_copy(lax.rem(mine + k, n_exp), mine).start()
-
-    weights_in[mine] = slot_weights[turned_index(mine)]
-
+    ahead = window + LEAD
     place_copy().wait_recv()
     for c in range(window):
         send_slots(c)
+
+    @pl.loop(0, chunks)
+    def _(c):
+        proj_copy(c).start()
 
     @pl.loop(1, n_exp)
     def _(k):
@@ -691,7 +607,7 @@
             def _(q):
                 query_copy(q, chip).start()
 
-        @pl.when(c == chunks - 1)
+        @pl.when(c == chunks)
         def _():
             all_through = through[...]
             act_out[...] = (all_through * slot_weight).astype(BF16)
@@ -755,10 +671,160 @@
         z_copy(c).wait_send()
 
 
-def experts(stream_total, query_parts, ids, route, acts, proj, key_width, query_rows):
+def layer_kernel(sizes, *refs):
+    attention_sizes, expert_sizes, shapes, counts = sizes
+    refs = list(refs)
+
+    def take(n):
+        taken = refs[:n]
+        del refs[:n]
+        return taken
+
+    queries, out_grad, latents_t, gain, hidden, stream, proj_t, ids, route, acts, proj = take(11)
+    stream_out, act_out, down_out, weight_out, query_out = take(5)
+    rows_all, stats_all, key_all, query_parts = take(4)
+    placing, peer_placing, peer_rows, slot_weights, returned, query_in, query_sum, query_all = take(8)
+    arrived, weights_in, core_in, x_in, z_in, slot_parts = take(6)
+    attention_sems = take(counts[0])
+    expert_sems = take(counts[1])
+    greet((("ctx", attention_sizes[0]), ("exp", attention_sizes[1])))
+
+    n_exp, chunks, window = attention_sizes[1], expert_sizes[2], expert_sizes[6]
+    mine = lax.axis_index("exp")
+    l_at = lax.rem(mine, 2)
+    partner = {"exp": mine + 1 - 2 * l_at}
+    depth = stream_out.shape[1] // chunks
+    place_send, place_recv, peer_send, peer_recv = expert_sems[1:5]
+    weight_send, weight_recv = expert_sems[7:9]
+
+    def row_of(e):
+        return lax.rem(e, 2) * (n_exp // 2) + e // 2
+
+    def place_copy():
+        return push(placing.at[1 - l_at], peer_placing, place_send.at[0], place_recv.at[0], partner)
+
+    def rows_copy(c):
+        columns = pl.ds(pl.multiple_of(c * depth, depth), depth)
+        return push(stream_out.at[:, columns], peer_rows.at[c], peer_send.at[c], peer_recv.at[c], partner)
+
+    def weight_copy(there, source):
+        return push(
+            slot_weights.at[row_of(there)],
+            weights_in.at[source],
+            weight_send.at[there],
+            weight_recv.at[source],
+            {"exp": there},
+        )
+
+    def idle():
+        slot_tables(ids, route, placing, slot_weights)
+        place_copy().start()
+
+        @pl.loop(1, n_exp)
+        def _(k):
+            weight_copy(lax.rem(mine + k, n_exp), mine).start()
+
+        weights_in[mine] = slot_weights[row_of(mine)]
+
+    def ready(c):
+        @pl.when(c < window + LEAD)
+        def _():
+            rows_copy(c).start()
+
+    def first(keys, weights, grads, score_grads, key_parts, hidden_in, stream_in, proj_t_in):
+        attention_part(
+            attention_sizes,
+            idle,
+            ready,
+            queries,
+            out_grad,
+            latents_t,
+            gain,
+            hidden,
+            stream,
+            proj_t,
+            stream_out,
+            query_parts,
+            rows_all,
+            stats_all,
+            keys,
+            weights,
+            grads,
+            score_grads,
+            key_parts,
+            key_all,
+            hidden_in,
+            stream_in,
+            proj_t_in,
+            *attention_sems,
+        )
+
+    def second(proj_in, outgoing, acts_t, through, partial, z_part):
+        expert_part(
+            expert_sizes,
+            place_copy,
+            rows_copy,
+            weight_copy,
+            stream_out,
+            query_parts,
+            ids,
+            acts,
+            proj,
+            act_out,
+            down_out,
+            weight_out,
+            query_out,
+            proj_in,
+            placing,
+            peer_placing,
+            peer_rows,
+            slot_weights,
+            returned,
+            query_in,
+            query_sum,
+            query_all,
+            outgoing,
+            arrived,
+            weights_in,
+            acts_t,
+            through,
+            partial,
+            core_in,
+            x_in,
+            z_part,
+            z_in,
+            slot_parts,
+            *expert_sems,
+        )
+
+    pl.run_scoped(first, *shapes[0])
+    pl.run_scoped(second, *shapes[1])
+
+
+def layer(
+    queries,
+    latents,
+    out_grad,
+    hidden_rows,
+    norm_gain,
+    latent_proj,
+    stream_grad,
+    ids,
+    route,
+    acts,
+    proj,
+):
     n_ctx, n_exp = lax.axis_size("ctx"), lax.axis_size("exp")
+    key_count, key_width = latents.shape
+    query_rows = queries.shape[0]
+    heads = queries.shape[1] // key_width
+    value_width = out_grad.shape[1] // heads
+    per = query_rows * heads
+    wide = padded(key_width)
+    piece = key_count // n_exp
+    total_rows = n_ctx * per
+    tokens, width = hidden_rows.shape
     slots, inner = acts.shape
-    tokens, width = stream_total.shape
     top_count = ids.shape[1]
     capacity = slots // n_exp
     chunks = 10
@@ -767,67 +833,140 @@
     depth = width // chunks
     share = inner // n_ctx
     chips = n_ctx // 2
-    per, wide = query_parts.shape[2:]
+    half = n_exp // 2
     vmem = pl.BlockSpec(memory_space=pltpu.VMEM)
+    hbm = pl.BlockSpec(memory_space=pl.ANY)
     dma = pltpu.SemaphoreType.DMA
-    sizes = (n_ctx, n_exp, chunks, n_x, n_z, key_width, 3, (1, 3, 5))
+    attention_sizes = (n_ctx, n_exp, key_width, value_width, query_rows, heads, chunks)
+    expert_sizes = (n_ctx, n_exp, chunks, n_x, n_z, key_width, 3, (1, 3, 5))
+    first = (
+        pltpu.VMEM((key_count, wide), BF16),
+        pltpu.VMEM((key_count, total_rows), F32),
+        pltpu.VMEM((key_count, total_rows), F32),
+        pltpu.VMEM((key_count, total_rows), BF16),
+        pltpu.VMEM((n_exp, piece, wide), BF16),
+        pltpu.VMEM((tokens, width), BF16),
+        pltpu.VMEM((tokens, width), BF16),
+        pltpu.VMEM((wide, width), BF16),
+    )
+    second = (
+        pltpu.VMEM((chunks, inner, depth), BF16),
+        pltpu.VMEM((chunks, 2, half, capacity, depth), BF16),
+        pltpu.VMEM((inner, slots), BF16),
+        pltpu.VMEM((slots, inner), F32),
+        pltpu.VMEM((chunks, 2, n_x, n_z, share, depth), BF16),
+        pltpu.VMEM((chunks, n_z, share, depth), BF16),
+    )
+    held = [
+        pltpu.VMEM((n_ctx, per, wide + value_width), BF16),
+        pltpu.VMEM((n_ctx, 3, total_rows // LANES, LANES), F32),
+        pltpu.VMEM((n_exp, piece, wide), BF16),
+        pltpu.VMEM((2, chips, per, wide), BF16),
+        pltpu.VMEM((2, slots // 2, tokens), BF16),
+        pltpu.VMEM((slots // 2, tokens), BF16),
+        pltpu.VMEM((chunks, tokens, depth), BF16),
+        pltpu.VMEM((n_exp, capacity, LANES), BF16),
+        pltpu.VMEM((n_exp, capacity, LANES), F32),
+        pltpu.VMEM((chips, per, wide), BF16),
+        pltpu.VMEM((chips, per, wide), BF16),
+        pltpu.VMEM((chips, per, wide), BF16),
+        pltpu.VMEM((chunks, n_exp, capacity, depth), BF16),
+        pltpu.VMEM((n_exp, capacity, LANES), BF16),
+        pltpu.VMEM((chunks, n_x, n_z, share, depth), BF16),
+        pltpu.VMEM((chunks, n_x, n_z, share, depth), BF16),
+        pltpu.VMEM((chunks, share, depth), BF16),
+        pltpu.VMEM((n_exp, capacity, LANES), F32),
+    ]
+    attention_sems = [
+        dma((3,)),
+        dma((n_ctx,)),
+        dma((n_ctx,)),
+        dma((n_ctx,)),
+        dma((n_ctx,)),
+        dma((n_ctx,)),
+        dma((n_exp,)),
+        dma((n_exp,)),
+    ]
+    expert_sems = [
+        dma((chunks,)),
+        dma((1,)),
+        dma((1,)),
+        dma((chunks,)),
+        dma((chunks,)),
+        dma((chunks, 2, half)),
+        dma((chunks, n_exp)),
+        dma((n_exp,)),
+        dma((n_exp,)),
+        dma((chunks,)),
+        dma((chunks,)),
+        dma((chunks, n_x)),
+        dma((chunks, n_x)),
+        dma((chunks,)),
+        dma((chunks,)),
+        dma((n_exp,)),
+        dma((n_exp,)),
+        dma((1,)),
+        dma((1,)),
+        dma((chips,)),
+        dma((chips,)),
+    ]
+    counts = (len(attention_sems), len(expert_sems))
+    sizes = (attention_sizes, expert_sizes, (first, second), counts)
     return pl.pallas_call(
-        functools.partial(expert_kernel, sizes),
+        functools.partial(layer_kernel, sizes),
         out_shape=(
+            jax.ShapeDtypeStruct((tokens, width), BF16),
             jax.ShapeDtypeStruct((slots, inner), BF16),
             jax.ShapeDtypeStruct((share, width), BF16),
             jax.ShapeDtypeStruct((top_count, tokens), F32),
-            jax.ShapeDtypeStruct((query_rows, per // query_rows * key_width), BF16),
+            jax.ShapeDtypeStruct((query_rows, heads * key_width), BF16),
         ),
-        in_specs=[vmem, vmem, vmem, vmem, vmem, pl.BlockSpec(memory_space=pl.ANY)],
-        out_specs=(vmem, vmem, vmem, vmem),
-        scratch_shapes=[
-            pltpu.VMEM((chunks, inner, depth), BF16),
-            pltpu.VMEM((2, slots // 2, tokens), BF16),
-            pltpu.VMEM((slots // 2, tokens), BF16),
-            pltpu.VMEM((chunks, tokens, depth), BF16),
-            pltpu.VMEM((n_exp, capacity, LANES), BF16),
-            pltpu.VMEM((n_exp, capacity, LANES), F32),
-            pltpu.VMEM((chips, per, wide), BF16),
-            pltpu.VMEM((chips, per, wide), BF16),
-            pltpu.VMEM((chips, per, wide), BF16),
-            pltpu.VMEM((chunks, 2, n_exp // 2, capacity, depth), BF16),
-            pltpu.VMEM((chunks, n_exp, capacity, depth), BF16),
-            pltpu.VMEM((n_exp, capacity, LANES), BF16),
-            pltpu.VMEM((inner, slots), BF16),
-            pltpu.VMEM((slots, inner), F32),
-            pltpu.VMEM((chunks, 2, n_x, n_z, share, depth), BF16),
-            pltpu.VMEM((chunks, n_x, n_z, share, depth), BF16),
-            pltpu.VMEM((chunks, n_x, n_z, share, depth), BF16),
-            pltpu.VMEM((chunks, n_z, share, depth), BF16),
-            pltpu.VMEM((chunks, share, depth), BF16),
-            pltpu.VMEM((n_exp, capacity, LANES), F32),
-            dma((chunks,)),
-            dma((1,)),
-            dma((1,)),
-            dma((chunks,)),
-            dma((chunks,)),
-            dma((chunks, 2, n_exp // 2)),
-            dma((chunks, n_exp)),
-            dma((n_exp,)),
-            dma((n_exp,)),
-            dma((chunks,)),
-            dma((chunks,)),
-            dma((chunks, n_x)),
-            dma((chunks, n_x)),
-            dma((chunks,)),
-            dma((chunks,)),
-            dma((n_exp,)),
-            dma((n_exp,)),
-            dma((1,)),
-            dma((1,)),
-            dma((chips,)),
-            dma((chips,)),
-        ],
+        in_specs=[vmem, vmem, vmem, vmem, hbm, hbm, hbm, vmem, vmem, vmem, hbm],
+        out_specs=(vmem, vmem, vmem, vmem, vmem),
+        scratch_shapes=held + attention_sems + expert_sems,
         compiler_params=pltpu.CompilerParams(
-            collective_id=1, has_side_effects=True, vmem_limit_bytes=61 * 2**20
+            collective_id=0, has_side_effects=True, vmem_limit_bytes=62 * 2**20
         ),
-    )(stream_total, query_parts, ids.T, route.T, acts, proj)
+    )(
+        queries,
+        out_grad,
+        latents.T,
+        norm_gain.reshape(1, width),
+        hidden_rows,
+        stream_grad,
+        latent_proj.T,
+        ids.T,
+        route.T,
+        acts,
+        proj,
+    )
+
+
+def settle_kernel(*refs):
+    count = (len(refs) - 2) // 3
+    arrays, results, held = refs[:count], refs[count : 2 * count], refs[2 * count : 3 * count]
+    in_sem, out_sem = refs[-2:]
+    loads = [pltpu.make_async_copy(arrays[n], held[n], in_sem.at[n]) for n in range(count)]
+    stores = [pltpu.make_async_copy(held[n], results[n], out_sem.at[n]) for n in range(count)]
+    for n in range(count):
+        loads[n].start()
+    for n in range(count):
+        loads[n].wait()
+        stores[n].start()
+    for n in range(count):
+        stores[n].wait()
+
+
+def settle(*arrays):
+    hbm = pl.BlockSpec(memory_space=pl.ANY)
+    sems = [pltpu.SemaphoreType.DMA((len(arrays),))] * 2
+    return pl.pallas_call(
+        settle_kernel,
+        out_shape=tuple(jax.ShapeDtypeStruct(a.shape, a.dtype) for a in arrays),
+        in_specs=[hbm] * len(arrays),
+        out_specs=(hbm,) * len(arrays),
+        scratch_shapes=[pltpu.VMEM(a.shape, a.dtype) for a in arrays] + sems,
+    )(*arrays)
 
 
 def body(
@@ -843,18 +982,21 @@
     expert_acts,
     down_proj,
 ):
-    stream_total, query_parts = attention(
-        queries, latents, out_grad, hidden_rows, norm_gain, latent_proj, stream_grad
-    )
-    act_grad, down_share, weight_grad, query_grad = experts(
-        stream_total,
-        query_parts,
+    stream_total, act_grad, down_share, weight_grad, query_grad = layer(
+        queries,
+        latents,
+        out_grad,
+        hidden_rows,
+        norm_gain,
+        latent_proj,
+        stream_grad,
         expert_ids,
         route_weights,
         expert_acts[0],
         down_proj[0],
-        latents.shape[1],
-        queries.shape[0],
+    )
+    stream_total, act_grad, down_share, query_grad = settle(
+        stream_total, act_grad, down_share, query_grad
     )
     return (query_grad, stream_total, act_grad[None], down_share[None], weight_grad.T)
 

time: 158 us -> 149 us (0.943); the launches traced: 158 us -> 146 us
  Pallas kernels: 151 us -> 145 us
  local copies, waits for them, and re-layouts: 5.79 us -> 0.57 us
    pallas_call x2, Pallas kernels: 151 us -> 145 us  [the longest x1 142 us: layer(): pl.pallas_call(functools.partial(layer_kernel, sizes), out_shape=(jax.Sha...]
    unnamed x13 -> x3, local copies, waits for them, and re-layouts: 5.79 us -> 0.57 us
where the time goes in v5:
time: 149 us; the launch traced here: 146 us
  Pallas kernels  145 us (97%)
    pallas_call x1, Pallas kernels, layer(): pl.pallas_call(functools.partial(layer_kernel, sizes), out_shape=(jax.Sha...  142 us

profile of v5, /device:TPU:0, one launch (start us, length us, event | category | flops | bytes accessed | tf_op | source)
XLA Modules:
  0.0 146.4 jit_solution(8464220688354798365)
XLA Ops:
  0.6 142.3 %shard_map.146 = (bf16[128,5120]{1,0:T(8,128)(2,1)}, bf16[512,768]{1,0:T(8,128)(2,1)}, bf16[48,5120]{1,0:T(8,128)(2,1)}, f32[2,128]{1,0:T(2,128)}, bf16[8,4608]{1,0:T(8,128)(2,1)}) custom-call(bf16[8,4608]{1,0:T(8,128)(2,1)} %refs_0_.1, bf16[8,4096]{1,0:T(8,128)(2,1)} %refs_1_.1, bf16[576,1024]{1,0:T(8,128)(2,1)} %bitcast.12, f32[1,5120]{1,0:T(1,128)} %bitcast.14, ...), custom_call_target="tpu_custom_call" | custom-call | tf_op jit(solution)/shard_map/pallas_call | solution.py:915
  142.9 0.0 copy-start
  142.9 2.9 %shard_map.147 = (bf16[128,5120]{1,0:T(8,128)(2,1)}, bf16[512,768]{1,0:T(8,128)(2,1)}, bf16[48,5120]{1,0:T(8,128)(2,1)}, bf16[8,4608]{1,0:T(8,128)(2,1)}) custom-call(bf16[128,5120]{1,0:T(8,128)(2,1)} %get-tuple-element.14.refs_0_, bf16[512,768]{1,0:T(8,128)(2,1)} %get-tuple-element.15.refs_1_, bf16[48,5120]{1,0:T(8,128)(2,1)} %get-tuple-element.16.refs_2_, ...), custom_call_target="tpu_custom_call" | custom-call | tf_op jit(solution)/shard_map/pallas_call | solution.py:963
  145.8 0.0 copy-done
  145.8 0.6 copy.17
Async XLA Ops:
  142.9 2.9 %copy-start = (f32[2,128]{1,0:T(2,128)S(1)}, f32[2,128]{1,0:T(2,128)}, u32[]{:S(2)}) copy-start(f32[2,128]{1,0:T(2,128)} %get-tuple-element.22) | copy-start | bytes 3076

commit v6 on v5

--- a/solution.py
+++ b/solution.py
@@ -73,6 +73,8 @@
     hidden,
     stream,
     proj_t,
+    squares,
+    pulled_t,
     load_sem,
     rows_send,
     rows_recv,
@@ -191,6 +193,22 @@
             for n, value in enumerate((top, total, dotted)):
                 stats_all[me, n, pl.ds(g * tiles + k, 1)] = value[:, part]
 
+    span = width // n_groups
+    tokens = hidden.shape[0]
+    squares[...] = jnp.zeros(squares.shape, F32)
+    pulled_t[...] = jnp.zeros(pulled_t.shape, F32)
+
+    def pull(n):
+        at = pl.ds(pl.multiple_of(n * span, span), span)
+        values = hidden[:, at].astype(F32)
+        squares[...] += jnp.broadcast_to(
+            jnp.sum(values * values, axis=1, keepdims=True), squares.shape
+        )
+        gained = values * gain_ref[:, at]
+        high = gained.astype(BF16)
+        low = (gained - high.astype(F32)).astype(BF16)
+        pulled_t[...] += nt_dot(proj_t[:, at], jnp.concatenate([high, low], axis=0))
+
     @pl.loop(first, n_groups + 1)
     def _(g):
         @pl.when(g < n_groups)
@@ -219,15 +237,6 @@
     @pl.loop(1, n_ctx)
     def _(i):
         stats_copy(lax.rem(me + i, n_ctx), me).start()
-
-    hidden_load.wait()
-    proj_load.wait()
-    hidden_values = hidden[...].astype(F32)
-    inverse = lax.rsqrt(jnp.mean(hidden_values * hidden_values, axis=1, keepdims=True) + EPSILON)
-    gained = hidden_values * gain_ref[...]
-    high = gained.astype(BF16)
-    low = (gained - high.astype(F32)).astype(BF16)
-    pulled = (nt_dot(high, proj_t[...]) + nt_dot(low, proj_t[...])) * (1.0 / width)
 
     @pl.loop(0, n_ctx)
     def _(i):
@@ -275,6 +284,12 @@
                 key_copy(2 * n + k, mine).start()
 
     key_all[mine] = key_parts[mine]
+    hidden_load.wait()
+    proj_load.wait()
+
+    @pl.loop(0, n_groups)
+    def _(n):
+        pull(n)
 
     @pl.loop(0, n_groups)
     def _(g):
@@ -283,6 +298,9 @@
         parts = part.astype(BF16).reshape(group, per, wide)
         for k in range(group):
             query_out[k % 2, g * (group // 2) + k // 2] = parts[k]
+
+    inverse = lax.rsqrt(squares[:, :1] * (1.0 / width) + EPSILON)
+    pulled = (pulled_t[:, :tokens] + pulled_t[:, tokens:]).T * (1.0 / width)
 
     @pl.loop(0, n_exp)
     def _(s):
@@ -731,7 +749,9 @@
         def _():
             rows_copy(c).start()
 
-    def first(keys, weights, grads, score_grads, key_parts, hidden_in, stream_in, proj_t_in):
+    def first(
+        keys, weights, grads, score_grads, key_parts, hidden_in, stream_in, proj_t_in, squares, pulled_t
+    ):
         attention_part(
             attention_sizes,
             idle,
@@ -756,6 +776,8 @@
             hidden_in,
             stream_in,
             proj_t_in,
+            squares,
+            pulled_t,
             *attention_sems,
         )
 
@@ -848,6 +870,8 @@
         pltpu.VMEM((tokens, width), BF16),
         pltpu.VMEM((tokens, width), BF16),
         pltpu.VMEM((wide, width), BF16),
+        pltpu.VMEM((tokens, LANES), F32),
+        pltpu.VMEM((wide, 2 * tokens), F32),
     )
     second = (
         pltpu.VMEM((chunks, inner, depth), BF16),
@@ -995,9 +1019,7 @@
         expert_acts[0],
         down_proj[0],
     )
-    stream_total, act_grad, down_share, query_grad = settle(
-        stream_total, act_grad, down_share, query_grad
-    )
+    stream_total, act_grad, down_share = settle(stream_total, act_grad, down_share)
     return (query_grad, stream_total, act_grad[None], down_share[None], weight_grad.T)
 
 

time: 149 us -> 149 us (level)
  no operation moved by 1% of the time
where the time goes in v6:
time: 149 us; the launch traced here: 147 us
  Pallas kernels  145 us (97%)
    pallas_call x1, Pallas kernels, layer(): pl.pallas_call(functools.partial(layer_kernel, sizes), out_shape=(jax.Sha...  142 us

profile of v6, /device:TPU:0, one launch (start us, length us, event | category | flops | bytes accessed | tf_op | source)
XLA Modules:
  0.0 147.0 jit_solution(14168319461800906874)
XLA Ops:
  0.6 142.3 %shard_map.146 = (bf16[128,5120]{1,0:T(8,128)(2,1)}, bf16[512,768]{1,0:T(8,128)(2,1)}, bf16[48,5120]{1,0:T(8,128)(2,1)}, f32[2,128]{1,0:T(2,128)}, bf16[8,4608]{1,0:T(8,128)(2,1)}) custom-call(bf16[8,4608]{1,0:T(8,128)(2,1)} %refs_0_.1, bf16[8,4096]{1,0:T(8,128)(2,1)} %refs_1_.1, bf16[576,1024]{1,0:T(8,128)(2,1)} %bitcast.12, f32[1,5120]{1,0:T(1,128)} %bitcast.14, ...), custom_call_target="tpu_custom_call" | custom-call | tf_op jit(solution)/shard_map/pallas_call | solution.py:939
  142.9 0.0 copy-start
  142.9 0.0 copy-start.1
  142.9 2.9 %shard_map.147 = (bf16[128,5120]{1,0:T(8,128)(2,1)}, bf16[512,768]{1,0:T(8,128)(2,1)}, bf16[48,5120]{1,0:T(8,128)(2,1)}) custom-call(bf16[128,5120]{1,0:T(8,128)(2,1)} %get-tuple-element.14.refs_0_, bf16[512,768]{1,0:T(8,128)(2,1)} %get-tuple-element.15.refs_1_, bf16[48,5120]{1,0:T(8,128)(2,1)} %get-tuple-element.16.refs_2_), custom_call_target="tpu_custom_call" | custom-call | tf_op jit(solution)/shard_map/pallas_call | solution.py:987
  145.8 0.0 copy-done
  145.8 0.6 copy.18
  146.4 0.0 copy-done.1
  146.4 0.6 copy.19
Async XLA Ops:
  142.9 2.9 %copy-start = (bf16[8,4608]{1,0:T(8,128)(2,1)S(1)}, bf16[8,4608]{1,0:T(8,128)(2,1)}, u32[]{:S(2)}) copy-start(bf16[8,4608]{1,0:T(8,128)(2,1)} %get-tuple-element.26) | copy-start | bytes 221188
  142.9 3.5 %copy-start.1 = (f32[2,128]{1,0:T(2,128)S(1)}, f32[2,128]{1,0:T(2,128)}, u32[]{:S(2)}) copy-start(f32[2,128]{1,0:T(2,128)} %get-tuple-element.20) | copy-start | bytes 3076
